TPU v7x, 32 devices: a whole 2x2x4 slice. The times are simulated.
32 devices in a mesh: dp: 8 (over z, x), group: 4 (over y, core).
Axes of the slice: x: 2, y: 2, z: 4, core: 2. Of those that a mesh axis runs over, the one named last changes fastest.
Arguments:
- hidden_in: bfloat16 [16, 256, 576], P('dp', 'group'), may hold values from -4 to 4
- out_grad: bfloat16 [16, 256, 576], P('dp', 'group'), may hold values from -6 to 6
- span_order: int32 [16, 8], P('dp'), may hold values from 0 to 7, each once within a row
- weights: float32 [3538944], P('group'), may hold values from -2 to 2
- first_moment: float32 [3538944], P('group'), may hold values from -30 to 30
- second_moment: float32 [3538944], P('group'), may hold values from 10 to 1000
- gains: float32 [2, 576], P(None, 'group'), may hold values from 0.5 to 1.5
- gain_first: float32 [2, 576], P(None, 'group'), may hold values from -30 to 30
- gain_second: float32 [2, 576], P(None, 'group'), may hold values from 10 to 1000
Outputs:
- block_out: float32 [16, 256, 576], P('dp', 'group')
- in_grad: float32 [16, 256, 576], P('dp', 'group')
- weight_grad: float32 [3538944], P('group')
- gain_grad: float32 [2, 576], P(None, 'group')
- new_weights: float32 [3538944], P('group')
- new_first: float32 [3538944], P('group')
- new_second: float32 [3538944], P('group')
- new_gains: float32 [2, 576], P(None, 'group')
- new_gain_first: float32 [2, 576], P(None, 'group')
- new_gain_second: float32 [2, 576], P(None, 'group')
Inputs may be any that keep to these rules, and one draw needn't show every extreme that they name: Each row of span_order is a permutation of the 8 blocks of positions of its sequence.
All inputs are finite; a program needn't handle non-finite values.
Results may differ from a plain program's by a relative error of at most 0.014.
The roundings to bfloat16 on the way count: a program that leaves them out, or rounds other values in their place, can miss the bound.
Values may be sent and summed in bfloat16 or wider, within the bound.
A program may use at most 128 MiB of HBM per device.

v0:
```python
import jax
import jax.numpy as jnp
from jax import lax
from jax.sharding import PartitionSpec as P

D = 576
HEADS = 9
KV_HEADS = 3
HEAD_DIM = 64
FF = 1536
SPAN = 32


EPS_NORM = 1e-05
ROPE_BASE = 100000.0
BETA_ONE = 0.9
BETA_TWO = 0.95
LEARN_RATE = 0.02
GAIN_RATE = 0.25
DECAY_RATE = 0.1
EPS_ADAM = 1e-08
CORRECT_ONE = 1.0 - 0.9**5
CORRECT_TWO = 1.0 - 0.95**5
NEG_LARGE = -1e30


def split_weights(flat_vector):
    q_width = HEADS * HEAD_DIM
    kv_width = KV_HEADS * HEAD_DIM
    layout = [(D, q_width), (D, kv_width), (D, kv_width), (q_width, D), (D, FF), (D, FF), (FF, D)]
    pieces = []
    offset = 0
    for rows_cols in layout:
        amount = rows_cols[0] * rows_cols[1]
        pieces.append(
            lax.slice_in_dim(flat_vector, offset, offset + amount, axis=0).reshape(rows_cols)
        )
        offset = offset + amount
    return pieces


def rope_tables(positions):
    freq_index = jnp.arange(HEAD_DIM // 2, dtype=jnp.float32)
    inverse = ROPE_BASE ** (-2.0 * freq_index / HEAD_DIM)
    angles = positions.astype(jnp.float32)[:, None] * inverse[None, :]
    return (jnp.cos(angles), jnp.sin(angles))


def rotate(vectors, cosine, sine_table):
    half_dim = HEAD_DIM // 2
    first_half = vectors[..., :half_dim]
    second_half = vectors[..., half_dim:]
    cos_b = cosine[:, None, :]
    sin_b = sine_table[:, None, :]
    return jnp.concatenate(
        [first_half * cos_b - second_half * sin_b, second_half * cos_b + first_half * sin_b],
        axis=-1,
    )


def rotate_back(vectors, cosine, sine_table):
    half_dim = HEAD_DIM // 2
    first_half = vectors[..., :half_dim]
    second_half = vectors[..., half_dim:]
    cos_b = cosine[:, None, :]
    sin_b = sine_table[:, None, :]
    return jnp.concatenate(
        [first_half * cos_b + second_half * sin_b, second_half * cos_b - first_half * sin_b],
        axis=-1,
    )


def norm_forward(vectors):
    factor = lax.rsqrt(jnp.mean(vectors * vectors, axis=-1, keepdims=True) + EPS_NORM)
    return (vectors * factor, factor)


def norm_backward(grad_normed, normed, factor):
    return factor * (grad_normed - normed * jnp.mean(grad_normed * normed, axis=-1, keepdims=True))


def outer_sum(left_rows, right_rows):
    return lax.dot_general(
        left_rows, right_rows, (((0,), (0,)), ((), ())), preferred_element_type=jnp.float32
    )


def adamw_step(param_now, moment_one, moment_two, grad_now, decay_weight, step_rate):
    first_new = BETA_ONE * moment_one + (1.0 - BETA_ONE) * grad_now
    second_new = BETA_TWO * moment_two + (1.0 - BETA_TWO) * grad_now * grad_now
    update = first_new / CORRECT_ONE / (jnp.sqrt(second_new / CORRECT_TWO) + EPS_ADAM)
    return (param_now - step_rate * (update + decay_weight * param_now), first_new, second_new)


def split_pair(kv_seq):
    kv_width = KV_HEADS * HEAD_DIM
    key_blk = kv_seq[:, :kv_width].reshape(-1, KV_HEADS, HEAD_DIM)
    value_blk = kv_seq[:, kv_width:].reshape(-1, KV_HEADS, HEAD_DIM)
    return (key_blk, value_blk)


def masked_scores(query_blk, key_blk, query_pos, key_pos):
    scores = jnp.einsum(
        "qkgd,skd->kgqs", query_blk, key_blk, preferred_element_type=jnp.float32
    ) * HEAD_DIM ** (-0.5)
    allowed = key_pos[None, :] <= query_pos[:, None]
    return jnp.where(allowed[None, None], scores, NEG_LARGE)


def attend(query_blk, kv_seq, query_pos, key_pos):
    key_blk, value_blk = split_pair(kv_seq)
    scores = masked_scores(query_blk, key_blk, query_pos, key_pos)
    row_max = jnp.max(scores, axis=-1)
    log_total = row_max + jnp.log(jnp.sum(jnp.exp(scores - row_max[..., None]), axis=-1))
    probs_b = jnp.exp(scores - log_total[..., None]).astype(jnp.bfloat16)
    attn_vals = jnp.einsum("kgqs,skd->qkgd", probs_b, value_blk, preferred_element_type=jnp.float32)
    return (attn_vals.reshape(attn_vals.shape[0], -1).astype(jnp.bfloat16), log_total)


def attend_back(query_blk, kv_seq, query_pos, key_pos, log_total, attn_rows, grad_rows):
    group_size = HEADS // KV_HEADS
    key_blk, value_blk = split_pair(kv_seq)
    scores = masked_scores(query_blk, key_blk, query_pos, key_pos)
    probs = jnp.exp(scores - log_total[..., None])
    probs_b = probs.astype(jnp.bfloat16)
    grad_heads = grad_rows.reshape(-1, KV_HEADS, group_size, HEAD_DIM)
    attn_heads = attn_rows.reshape(-1, KV_HEADS, group_size, HEAD_DIM)
    delta_rows = jnp.einsum(
        "qkgd,qkgd->kgq", grad_heads, attn_heads, preferred_element_type=jnp.float32
    )
    grad_probs = jnp.einsum(
        "qkgd,skd->kgqs", grad_heads, value_blk, preferred_element_type=jnp.float32
    )
    grad_scores = (probs * (grad_probs - delta_rows[..., None]) * HEAD_DIM ** (-0.5)).astype(
        jnp.bfloat16
    )
    grad_query = jnp.einsum(
        "kgqs,skd->qkgd", grad_scores, key_blk, preferred_element_type=jnp.float32
    )
    grad_key = jnp.einsum(
        "kgqs,qkgd->skd", grad_scores, query_blk, preferred_element_type=jnp.float32
    )
    grad_value = jnp.einsum(
        "kgqs,qkgd->skd", probs_b, grad_heads, preferred_element_type=jnp.float32
    )
    key_rows = grad_key.shape[0]
    stacked = jnp.concatenate(
        [grad_key.reshape(key_rows, -1), grad_value.reshape(key_rows, -1)], axis=-1
    )
    return (grad_query, stacked)


def body(
    hidden_in,
    out_grad,
    span_order,
    weights,
    first_moment,
    second_moment,
    gains,
    gain_first,
    gain_second,
):
    group_rank = lax.axis_index("group")
    seq_local = hidden_in.shape[0]
    slot_len = hidden_in.shape[1]
    width = hidden_in.shape[2]
    q_width = HEADS * HEAD_DIM
    kv_width = KV_HEADS * HEAD_DIM
    group_size = HEADS // KV_HEADS
    full_flat, full_gains = (
        lax.all_gather(weights.astype(jnp.bfloat16), "group", axis=0, tiled=True),
        lax.all_gather(gains.astype(jnp.bfloat16), "group", axis=1, tiled=True),
    )
    w_query, w_key, w_value, w_out, w_gate, w_up, w_down = split_weights(full_flat)
    gain_attn = full_gains[0].astype(jnp.float32)
    gain_ffn = full_gains[1].astype(jnp.float32)
    offsets = jnp.arange(SPAN, dtype=jnp.int32)
    all_pos = (span_order[:, :, None] * SPAN + offsets[None, None, :]).reshape(seq_local, -1)
    local_pos = lax.dynamic_slice_in_dim(all_pos, group_rank * slot_len, slot_len, 1)
    cosine, sine_table = rope_tables(local_pos.reshape(-1))
    residual = hidden_in.reshape(-1, width).astype(jnp.float32)
    normed_one, factor_one = norm_forward(residual)
    attn_in = (normed_one * gain_attn).astype(jnp.bfloat16)
    query_proj = jnp.dot(attn_in, w_query, preferred_element_type=jnp.float32).reshape(
        -1, HEADS, HEAD_DIM
    )
    key_proj = jnp.dot(attn_in, w_key, preferred_element_type=jnp.float32).reshape(
        -1, KV_HEADS, HEAD_DIM
    )
    value_proj = jnp.dot(attn_in, w_value, preferred_element_type=jnp.float32)
    query_b = rotate(query_proj, cosine, sine_table).astype(jnp.bfloat16)
    key_b = rotate(key_proj, cosine, sine_table).astype(jnp.bfloat16).reshape(-1, kv_width)
    value_b = value_proj.astype(jnp.bfloat16)
    kv_local = jnp.concatenate([key_b, value_b], axis=-1).reshape(seq_local, slot_len, 2 * kv_width)
    kv_all = lax.all_gather(kv_local, "group", axis=1, tiled=True)
    query_seq = query_b.reshape(seq_local, slot_len, KV_HEADS, group_size, HEAD_DIM)
    attn_parts = []
    lse_parts = []
    for seq_index in range(seq_local):
        attn_one, lse_one = attend(
            query_seq[seq_index], kv_all[seq_index], local_pos[seq_index], all_pos[seq_index]
        )
        attn_parts.append(attn_one)
        lse_parts.append(lse_one)
    attn_b = jnp.concatenate(attn_parts, axis=0)
    middle = residual + jnp.dot(attn_b, w_out, preferred_element_type=jnp.float32)
    normed_two, factor_two = norm_forward(middle)
    ffn_in = (normed_two * gain_ffn).astype(jnp.bfloat16)
    gate_proj = jnp.dot(ffn_in, w_gate, preferred_element_type=jnp.float32)
    up_proj = jnp.dot(ffn_in, w_up, preferred_element_type=jnp.float32)
    sigmoid_gate = jax.nn.sigmoid(gate_proj)
    hidden = (gate_proj * sigmoid_gate * up_proj).astype(jnp.bfloat16)
    block_out = middle + jnp.dot(hidden, w_down, preferred_element_type=jnp.float32)
    grad_out = out_grad.reshape(-1, width)
    gw_down = outer_sum(hidden, grad_out)
    grad_hidden = jnp.dot(grad_out, w_down.T, preferred_element_type=jnp.float32)
    grad_gate = (
        grad_hidden * up_proj * sigmoid_gate * (1.0 + gate_proj * (1.0 - sigmoid_gate))
    ).astype(jnp.bfloat16)
    grad_up = (grad_hidden * gate_proj * sigmoid_gate).astype(jnp.bfloat16)
    gw_gate = outer_sum(ffn_in, grad_gate)
    gw_up = outer_sum(ffn_in, grad_up)
    grad_ffn_in = jnp.dot(grad_gate, w_gate.T, preferred_element_type=jnp.float32) + jnp.dot(
        grad_up, w_up.T, preferred_element_type=jnp.float32
    )
    gg_ffn = jnp.sum(grad_ffn_in * normed_two, axis=0)
    grad_middle = grad_out.astype(jnp.float32) + norm_backward(
        grad_ffn_in * gain_ffn, normed_two, factor_two
    )
    grad_middle_b = grad_middle.astype(jnp.bfloat16)
    gw_out = outer_sum(attn_b, grad_middle_b)
    grad_attn = jnp.dot(grad_middle_b, w_out.T, preferred_element_type=jnp.float32).astype(
        jnp.bfloat16
    )
    kv_back = lax.all_gather(kv_local, "group", axis=1, tiled=True)
    attn_seq = attn_b.reshape(seq_local, slot_len, q_width)
    grad_attn_seq = grad_attn.reshape(seq_local, slot_len, q_width)
    query_grads = []
    kv_grads = []
    for seq_index in range(seq_local):
        grad_query_one, grad_kv_one = attend_back(
            query_seq[seq_index],
            kv_back[seq_index],
            local_pos[seq_index],
            all_pos[seq_index],
            lse_parts[seq_index],
            attn_seq[seq_index],
            grad_attn_seq[seq_index],
        )
        query_grads.append(grad_query_one)
        kv_grads.append(grad_kv_one)
    grad_query = jnp.concatenate(query_grads, axis=0).reshape(-1, HEADS, HEAD_DIM)
    grad_kv_all = jnp.stack(kv_grads)
    grad_kv = lax.psum_scatter(grad_kv_all, "group", scatter_dimension=1, tiled=True).reshape(
        -1, 2 * kv_width
    )
    grad_query_b = (
        rotate_back(grad_query, cosine, sine_table).reshape(-1, q_width).astype(jnp.bfloat16)
    )
    grad_key_b = (
        rotate_back(grad_kv[:, :kv_width].reshape(-1, KV_HEADS, HEAD_DIM), cosine, sine_table)
        .reshape(-1, kv_width)
        .astype(jnp.bfloat16)
    )
    grad_value_b = grad_kv[:, kv_width:].astype(jnp.bfloat16)
    gw_query = outer_sum(attn_in, grad_query_b)
    gw_key = outer_sum(attn_in, grad_key_b)
    gw_value = outer_sum(attn_in, grad_value_b)
    grad_attn_in = jnp.dot(grad_query_b, w_query.T, preferred_element_type=jnp.float32)
    grad_attn_in = grad_attn_in + jnp.dot(grad_key_b, w_key.T, preferred_element_type=jnp.float32)
    grad_attn_in = grad_attn_in + jnp.dot(
        grad_value_b, w_value.T, preferred_element_type=jnp.float32
    )
    gg_attn = jnp.sum(grad_attn_in * normed_one, axis=0)
    in_grad = grad_middle + norm_backward(grad_attn_in * gain_attn, normed_one, factor_one)
    flat_grad = jnp.concatenate(
        [
            grad_item.reshape(-1)
            for grad_item in (gw_query, gw_key, gw_value, gw_out, gw_gate, gw_up, gw_down)
        ]
    )
    gain_grad = jnp.stack([gg_attn, gg_ffn])
    grad_part, gain_part = (
        lax.psum_scatter(
            flat_grad.astype(jnp.bfloat16), "group", scatter_dimension=0, tiled=True
        ).astype(jnp.float32),
        lax.psum_scatter(
            gain_grad.astype(jnp.bfloat16), "group", scatter_dimension=1, tiled=True
        ).astype(jnp.float32),
    )
    grad_shard, gain_shard = lax.psum((grad_part, gain_part), "dp")
    new_weights, new_first, new_second = adamw_step(
        weights, first_moment, second_moment, grad_shard, DECAY_RATE, LEARN_RATE
    )
    new_gains, new_gain_first, new_gain_second = adamw_step(
        gains, gain_first, gain_second, gain_shard, 0.0, GAIN_RATE
    )
    return (
        block_out.reshape(seq_local, slot_len, width),
        in_grad.reshape(seq_local, slot_len, width),
        grad_shard,
        gain_shard,
        new_weights,
        new_first,
        new_second,
        new_gains,
        new_gain_first,
        new_gain_second,
    )


def solution(mesh):
    in_specs = (
        P("dp", "group", None),
        P("dp", "group", None),
        P("dp", None),
        P("group"),
        P("group"),
        P("group"),
        P(None, "group"),
        P(None, "group"),
        P(None, "group"),
    )
    out_specs = (
        P("dp", "group", None),
        P("dp", "group", None),
        P("group"),
        P(None, "group"),
        P("group"),
        P("group"),
        P("group"),
        P(None, "group"),
        P(None, "group"),
        P(None, "group"),
    )
    return jax.shard_map(body, mesh=mesh, in_specs=in_specs, out_specs=out_specs, check_vma=False)
```

profile of v0, /device:TPU:0, one launch (start us, length us, event | category | flops | bytes accessed | tf_op | source)
XLA Modules:
  0.0 466.2 jit_solution(7936541444893137600)
XLA Ops:
  7.3 3.5 convert_element_type.152
  11.0 6.0 %all-gather = bf16[4,144,2]{1,2,0:T(2,128)(2,1)S(1)} all-gather(bf16[1,144,2]{1,2,0:T(2,128)(2,1)S(1)} %convert_bitcast_fusion), channel_id=1, replica_groups=mesh['dp'=8,'group'=4] {'group'}, dimensions={0}, use_global_device_ids=true | all-gather | bytes 2880 | tf_op jit(solution)/shard_map/all_gather | solution.py:173
  19.8 44.7 %all-gather.3.cloned.1.call-done = bf16[3538944]{0:T(1024)(128)(2,1)} async-done(((bf16[884736]{0:T(1024)(128)(2,1)}), bf16[3538944]{0:T(1024)(128)(2,1)}) %all-gather.3.cloned.1.call-update) | async-done | bytes 7077904 | tf_op jit(solution)/shard_map/all_gather | solution.py:172
  70.0 6.5 %all_gather.12 = bf16[2,256,384]{2,0,1:T(2,128)(2,1)S(1)} all-gather(bf16[2,64,384]{2,0,1:T(2,128)(2,1)S(1)} %copy.66), channel_id=1, replica_groups=mesh['dp'=8,'group'=4] {'group'}, dimensions={1}, use_global_device_ids=true | all-gather | bytes 491520 | tf_op jit(solution)/shard_map/all_gather | solution.py:196
  84.0 5.0 %fusion.35 = (bf16[884736]{0:T(1024)(128)(2,1)}, bf16[884736]{0:T(1024)(128)(2,1)}, bf16[884736]{0:T(1024)(128)(2,1)}) fusion(bf16[3538944]{0:T(1024)(128)(2,1)} %all-gather.3.cloned.1.call-done), kind=kLoop, calls=%fused_computation.127 | loop fusion | bytes 10616832 | tf_op jit(solution)/shard_map/slice | solution.py:36
  89.1 3.8 slice.219
  92.8 3.6 slice.221
  97.6 1.4 fusion.47
  98.9 1.4 fusion.48
  100.3 4.3 slice.223
  104.6 3.6 multiply_convert_fusion
  119.2 1.6 convolution_convert_fusion.2
  120.8 3.2 reshape.450
  124.6 3.2 reshape.451
  127.8 1.9 convolution_convert_fusion
  129.7 2.8 copy.90
  132.5 3.2 reshape.452
  135.7 2.4 reduce-scatter.5.cloned.1.call-done
  139.1 2.0 convolution_convert_fusion.6
  147.7 1.4 constant_dynamic-update-slice_fusion.1
  153.0 1.5 multiply_reduce_fusion.2
  155.4 127.5 %all-reduce.6.cloned.1.call-done = bf16[3538944]{0:T(1024)(128)(2,1)} async-done(((bf16[3538944]{0:T(1024)(128)(2,1)}), bf16[3538944]{0:T(1024)(128)(2,1)}) %all-reduce.6.cloned.1.call-update) | async-done | bytes 7077904
  283.0 3.5 dynamic-slice_convert_fusion
  286.5 3.3 convolution_add_fusion.2
  289.9 1.9 copy.78
  292.4 2.0 multiply_add_fusion.1
  294.4 1.9 copy.87
  296.2 9.6 %reduce-scatter.7.cloned.1.call-done = bf16[144,2]{1,0:T(8,128)(2,1)} async-done(((bf16[576,2]{1,0:T(8,128)(2,1)}), bf16[144,2]{1,0:T(8,128)(2,1)}) %reduce-scatter.7.cloned.1.call-update) | async-done | bytes 592
  306.7 21.9 %psum.15 = f32[2,144]{1,0:T(2,128)S(1)} all-reduce(bf16[2,144]{1,0:T(2,128)(2,1)S(1)} %copy.122), channel_id=1, replica_groups=mesh['dp'=8,'group'=4] {'dp'}, use_global_device_ids=true, to_apply=%region_14.15 | all-reduce | flops 288 | bytes 1728 | tf_op jit(solution)/shard_map/psum | solution.py:292
  329.9 120.0 %all-reduce.4.cloned.1.call-done = f32[884736]{0:T(1024)} async-done(((f32[884736]{0:T(1024)}), f32[884736]{0:T(1024)}) %all-reduce.4.cloned.1.call-update) | async-done | bytes 3538960 | tf_op jit(solution)/shard_map/psum | solution.py:292
  449.9 7.7 %multiply_subtract_fusion = (f32[884736]{0:T(1024)}, f32[884736]{0:T(1024)}, f32[884736]{0:T(1024)}) fusion(f32[884736]{0:T(1024)S(1)} %copy-done.5, f32[884736]{0:T(1024)} %all-reduce.4.cloned.1.call-done, f32[884736]{0:T(1024)} %param.13, f32[884736]{0:T(1024)} %param.14), kind=kLoop, calls=%fused_computation.2 | loop fusion | flops 13271040 | bytes 24772608 | tf_op jit(solution)/shard_map/sub | solution.py:92
  457.7 2.0 copy.135
  (279 shorter events, 42.2 us)
Async XLA Ops:
  7.2 10.2 %copy-start.72 = (s32[2,8]{1,0:T(2,128)S(1)}, s32[2,8]{1,0:T(2,128)}, u32[]{:S(2)}) copy-start(s32[2,8]{1,0:T(2,128)} %param.11) | copy-start | bytes 196
  7.2 10.8 %copy-start.49 = (bf16[2,64,576]{2,1,0:T(8,128)(2,1)S(1)}, bf16[2,64,576]{2,1,0:T(8,128)(2,1)}, u32[]{:S(2)}) copy-start(bf16[2,64,576]{2,1,0:T(8,128)(2,1)} %param.10) | copy-start | bytes 442372
  7.2 57.3 %all-gather.3.cloned.1.call-start = ((), (), s32[]{:S(2)}) async-start(), calls=%async_computation.2 | async-start | bytes 8847360 | tf_op jit(solution)/shard_map/all_gather | solution.py:172
  10.8 127.4 %reduce-scatter.5.cloned.1.call-start = ((), (), s32[]{:S(2)}) async-start(), calls=%async_computation.3 | async-start | bytes 983040 | tf_op jit(solution)/shard_map/reduce_scatter | solution.py:255
  11.0 71.3 %copy-start.6 = (f32[128,576]{0,1:T(8,128)}, f32[128,576]{0,1:T(8,128)S(1)}, u32[]{:S(2)}) copy-start(f32[128,576]{0,1:T(8,128)S(1)} %copy.77) | copy-start | bytes 884740
  17.3 50.7 %copy-start.67 = (f32[128]{0:T(128)}, f32[128]{0:T(128)S(1)}, u32[]{:S(2)}) copy-start(f32[128]{0:T(128)S(1)} %rsqrt.21) | copy-start | bytes 1540
  19.4 48.6 %copy-start.56 = (f32[576]{0:T(1024)}, f32[576]{0:T(1024)S(1)}, u32[]{:S(2)}) copy-start(f32[576]{0:T(1024)S(1)} %get-tuple-element.25) | copy-start | bytes 6916
  19.6 59.1 %copy-start.54 = (f32[128,32]{0,1:T(8,128)}, f32[128,32]{0,1:T(8,128)S(1)}, u32[]{:S(2)}) copy-start(f32[128,32]{0,1:T(8,128)S(1)} %get-tuple-element.67) | copy-start | bytes 49156
  19.8 58.5 %copy-start.17 = (bf16[2,64,576]{2,1,0:T(8,128)(2,1)}, bf16[2,64,576]{2,1,0:T(8,128)(2,1)S(1)}, u32[]{:S(2)}) copy-start(bf16[2,64,576]{2,1,0:T(8,128)(2,1)S(1)} %multiply_convert_fusion.3) | copy-start | bytes 442372
  66.4 15.8 %copy-start.14 = (bf16[576,576]{1,0:T(8,128)(2,1)}, bf16[576,576]{1,0:T(8,128)(2,1)S(1)}, u32[]{:S(2)}) copy-start(bf16[576,576]{1,0:T(8,128)(2,1)S(1)} %slice.216) | copy-start | bytes 1990660
  78.9 4.6 copy-start.36
  79.9 9.1 %copy-start = (f32[3,3,64,256]{3,2,1,0:T(8,128)}, f32[3,3,64,256]{3,2,1,0:T(8,128)S(1)}, u32[]{:S(2)}) copy-start(f32[3,3,64,256]{3,2,1,0:T(8,128)S(1)} %get-tuple-element.69) | copy-start | bytes 1769476
  80.3 8.8 %copy-start.59 = (f32[3,3,64]{2,1,0:T(4,128)}, f32[3,3,64]{2,1,0:T(4,128)S(1)}, u32[]{:S(2)}) copy-start(f32[3,3,64]{2,1,0:T(4,128)S(1)} %log_add_fusion) | copy-start | bytes 6916
  80.5 8.6 %copy-start.42 = (bf16[256,192]{0,1:T(8,128)(2,1)}, bf16[256,192]{0,1:T(8,128)(2,1)S(1)}, u32[]{:S(2)}) copy-start(bf16[256,192]{0,1:T(8,128)(2,1)S(1)} %copy.68) | copy-start | bytes 294916
  81.3 7.7 %copy-start.61 = (f32[3,3,64]{2,1,0:T(4,128)}, f32[3,3,64]{2,1,0:T(4,128)S(1)}, u32[]{:S(2)}) copy-start(f32[3,3,64]{2,1,0:T(4,128)S(1)} %log_add_fusion.1) | copy-start | bytes 6916
  81.7 7.4 %copy-start.25 = (bf16[3,64,3,64]{3,1,2,0:T(8,128)(2,1)}, bf16[3,64,3,64]{3,1,2,0:T(8,128)(2,1)S(1)}, u32[]{:S(2)}) copy-start(bf16[3,64,3,64]{3,1,2,0:T(8,128)(2,1)S(1)} %convolution_convert_fusion.8) | copy-start | bytes 221188
  104.6 4.3 copy-start.70
  109.9 8.1 %copy-start.16 = (f32[128,576]{0,1:T(8,128)}, f32[128,576]{0,1:T(8,128)S(1)}, u32[]{:S(2)}) copy-start(f32[128,576]{0,1:T(8,128)S(1)} %multiply_add_fusion.2) | copy-start | bytes 884740
  114.7 168.3 %all-reduce.6.cloned.1.call-start = ((), (), s32[]{:S(2)}) async-start(), calls=%async_computation.6 | async-start | bytes 14155776
  118.4 5.6 %copy-start.30 = (bf16[128,1536]{1,0:T(8,128)(2,1)S(1)}, bf16[128,1536]{1,0:T(8,128)(2,1)}, u32[]{:S(2)}) copy-start(bf16[128,1536]{1,0:T(8,128)(2,1)} %copy-done.29) | copy-start | bytes 1179652
  129.7 9.3 %copy-start.7 = (f32[128,576]{0,1:T(8,128)S(1)}, f32[128,576]{0,1:T(8,128)}, u32[]{:S(2)}) copy-start(f32[128,576]{0,1:T(8,128)} %copy-done.6) | copy-start | bytes 884740
  129.7 9.4 %copy-start.57 = (f32[576]{0:T(1024)S(1)}, f32[576]{0:T(1024)}, u32[]{:S(2)}) copy-start(f32[576]{0:T(1024)} %copy-done.56) | copy-start | bytes 6916
  129.7 9.4 %copy-start.68 = (f32[128]{0:T(128)S(1)}, f32[128]{0:T(128)}, u32[]{:S(2)}) copy-start(f32[128]{0:T(128)} %copy-done.67) | copy-start | bytes 1540
  135.7 10.6 %copy-start.10 = (bf16[884736]{0:T(1024)(128)(2,1)S(1)}, bf16[884736]{0:T(1024)(128)(2,1)}, u32[]{:S(2)}) copy-start(bf16[884736]{0:T(1024)(128)(2,1)} %reshape.450) | copy-start | bytes 5308420
  150.5 155.4 %reduce-scatter.7.cloned.1.call-start = ((), (), s32[]{:S(2)}) async-start(), calls=%async_computation.5 | async-start | bytes 184320
  155.4 294.5 %all-reduce.4.cloned.1.call-start = ((), (), s32[]{:S(2)}) async-start(), calls=%async_computation.4 | async-start | bytes 7077888 | tf_op jit(solution)/shard_map/psum | solution.py:292
  286.5 5.9 %copy-start.58 = (f32[576]{0:T(1024)S(1)}, f32[576]{0:T(1024)}, u32[]{:S(2)}) copy-start(f32[576]{0:T(1024)} %copy-done.56) | copy-start | bytes 6916
  286.5 42.1 %copy-start.65 = (f32[2,144]{1,0:T(2,128)S(1)}, f32[2,144]{1,0:T(2,128)}, u32[]{:S(2)}) copy-start(f32[2,144]{1,0:T(2,128)} %param.15) | copy-start | bytes 3460
  286.5 42.1 %copy-start.71 = (f32[2,144]{1,0:T(2,128)S(1)}, f32[2,144]{1,0:T(2,128)}, u32[]{:S(2)}) copy-start(f32[2,144]{1,0:T(2,128)} %param.16) | copy-start | bytes 3460
  286.5 163.4 %copy-start.5 = (f32[884736]{0:T(1024)S(1)}, f32[884736]{0:T(1024)}, u32[]{:S(2)}) copy-start(f32[884736]{0:T(1024)} %param.12) | copy-start | bytes 10616836
  328.6 129.0 %copy-start.66 = (f32[2,144]{1,0:T(2,128)}, f32[2,144]{1,0:T(2,128)S(1)}, u32[]{:S(2)}) copy-start(f32[2,144]{1,0:T(2,128)S(1)} %psum.15) | copy-start | bytes 3460
  449.9 7.7 %copy-start.4 = (f32[884736]{0:T(1024)S(1)}, f32[884736]{0:T(1024)}, u32[]{:S(2)}) copy-start(f32[884736]{0:T(1024)} %all-reduce.4.cloned.1.call-done) | copy-start | bytes 10616836
  (47 other events, 102.5 us)
Sparse Core Ops, SparseCore 0:
  10.9 53.5 all-gather.2
  114.8 23.2 reduce-scatter.4
  150.6 132.3 all-reduce.5
  286.0 19.8 reduce-scatter.6
  310.3 139.5 all-reduce.3
where the time goes:
time: 467 us; the launch traced here: 466 us
  waiting for transfers between devices  304 us (65%)
  local copies, waits for them, and re-layouts  60.5 us (13%)
  blocking collectives  34.4 us (7%)
  matrix products  26.3 us (6%)
  other arithmetic  24.4 us (5%)
  between operations  15.8 us (3%)
    unnamed x7, waiting for transfers between devices  137 us
    psum x1, waiting for transfers between devices, body(): grad_shard, gain_shard = lax.psum((grad_part, gain_part), 'dp')  120 us
    all_gather x1, waiting for transfers between devices, body(): lax.all_gather(weights.astype(jnp.bfloat16), 'group', axis=0, tiled=True)  44.7 us
    psum x1, blocking collectives, body(): grad_shard, gain_shard = lax.psum((grad_part, gain_part), 'dp')  21.9 us
    slice x10, local copies, waits for them, and re-layouts, split_weights(): lax.slice_in_dim(flat_vector, offset, offset + amount, axis=0)  20.9 us
    unnamed x159, local copies, waits for them, and re-layouts  13.3 us
    reshape x7, local copies, waits for them, and re-layouts, body(): grad_item.reshape(-1)  11.9 us
  transfers between devices with their start and end apart: 5, of which 5 were waited for; matrix products, arithmetic and copies ran while one was open for 9% of the time, Pallas kernels for 0%

commit v1 on v0

--- a/solution.py
+++ b/solution.py
@@ -1,6 +1,10 @@
+import functools
+
 import jax
 import jax.numpy as jnp
 from jax import lax
+from jax.experimental import pallas as pl
+from jax.experimental.pallas import tpu as pltpu
 from jax.sharding import PartitionSpec as P
 
 D = 576
@@ -150,7 +154,403 @@
     return (grad_query, stacked)
 
 
+LANES = 128
+TILE = 16
+
+
+def cut_evenly(total_units, most):
+    count = max(1, min(most, total_units))
+    base, extra = divmod(total_units, count)
+    return [base + (1 if i < extra else 0) for i in range(count)]
+
+
+def block_of(rows):
+    for block in (144, 128, 96, 64, 48, 32):
+        if rows % block == 0:
+            return block
+    return TILE
+
+
+def over_rows(rows, step):
+    block = block_of(rows)
+    if rows == block:
+        step(0, block)
+        return
+
+    def one(i, carry):
+        step(pl.multiple_of(i * block, TILE), block)
+        return carry
+
+    lax.fori_loop(0, rows // block, one, 0)
+
+
+def rows_at(start, size):
+    return pl.ds(start if isinstance(start, int) else pl.multiple_of(start, TILE), size)
+
+
+class Copies:
+    def __init__(self, send_sem, recv_sem):
+        self.send_sem, self.recv_sem, self.made = send_sem, recv_sem, []
+
+    def start(self, src, dst, slot, where):
+        copy = pltpu.make_async_remote_copy(
+            src_ref=src,
+            dst_ref=dst,
+            send_sem=self.send_sem.at[slot],
+            recv_sem=self.recv_sem.at[slot],
+            device_id=where,
+            device_id_type=pl.DeviceIdType.MESH,
+        )
+        copy.start()
+        self.made.append(copy)
+
+    def arrived(self, dst, slot, where):
+        pltpu.make_async_remote_copy(
+            src_ref=dst,
+            dst_ref=dst,
+            send_sem=self.send_sem.at[slot],
+            recv_sem=self.recv_sem.at[slot],
+            device_id=where,
+            device_id_type=pl.DeviceIdType.MESH,
+        ).wait_recv()
+
+    def finish(self):
+        for copy in self.made:
+            copy.wait_send()
+
+
+def greet(targets):
+    barrier = pltpu.get_barrier_semaphore()
+    for where in targets:
+        pl.semaphore_signal(barrier, inc=1, device_id=where, device_id_type=pl.DeviceIdType.MESH)
+    pl.semaphore_wait(barrier, len(targets))
+
+
+def gather_kernel(n_group, n_dp, cuts, w_ref, g_ref, out_ref, gout_ref, send_sem, recv_sem):
+    me, dp = lax.axis_index("group"), lax.axis_index("dp")
+    core, chip, chips = me % 2, me // 2, n_group // 2
+    sib = me + 1 - 2 * core
+    half = dp % 2
+    pair = dp + 1 - 2 * half
+    half_rows = w_ref.shape[0] // 2
+    at = lambda rank, d: {"group": rank, "dp": d}
+    others = [(me + j) % n_group for j in range(1, n_group)]
+    greet([at(rank, dp) for rank in others] + [at(me, pair)])
+    copies = Copies(send_sem, recv_sem)
+    n_cut = len(cuts)
+    far = chips - 1
+    base_far = 0
+    base_pair = base_far + far * n_cut
+    base_near = base_pair + far * n_cut
+    base_near_pair = base_near + far * n_cut
+    base_own = base_near_pair + far * n_cut
+    base_gain = base_own + n_cut + 1
+    gout_ref[pl.ds(me, 1)] = g_ref[...][None]
+
+    def cast(start, rows):
+        def step(i, block):
+            out_ref[me, rows_at(start + i, block), :] = w_ref[
+                rows_at(start + i, block), :
+            ].astype(jnp.bfloat16)
+
+        over_rows(rows, step)
+
+    starts = []
+    start = 0
+    for rows in cuts:
+        starts.append(start)
+        start += rows
+    mine = half * half_rows
+    theirs = (1 - half) * half_rows
+    for c in range(n_cut):
+        cast(mine + starts[c], cuts[c])
+        piece = out_ref.at[me, rows_at(mine + starts[c], cuts[c]), :]
+        for j in range(1, chips):
+            to = ((chip + j) % chips) * 2 + core
+            copies.start(piece, piece, base_far + (j - 1) * n_cut + c, at(to, dp))
+        copies.start(piece, piece, base_own + c, at(sib, dp))
+    for j in range(1, n_group):
+        line = gout_ref.at[me]
+        copies.start(line, line, base_gain + j - 1, at((me + j) % n_group, dp))
+    cast(theirs, half_rows)
+    rest = out_ref.at[me, rows_at(theirs, half_rows), :]
+    copies.start(rest, rest, base_own + n_cut, at(sib, dp))
+    for c in range(n_cut + 1):
+        for j in range(1, chips):
+            source = ((chip + chips - j) % chips) * 2 + core
+            if c < n_cut:
+                piece = out_ref.at[source, rows_at(mine + starts[c], cuts[c]), :]
+                slot = (j - 1) * n_cut + c
+                copies.arrived(piece, base_far + slot, at(source, dp))
+                copies.start(piece, piece, base_pair + slot, at(me, pair))
+                copies.start(piece, piece, base_near + slot, at(sib, dp))
+            if c > 0:
+                piece = out_ref.at[source, rows_at(theirs + starts[c - 1], cuts[c - 1]), :]
+                slot = (j - 1) * n_cut + c - 1
+                copies.arrived(piece, base_pair + slot, at(me, pair))
+                copies.start(piece, piece, base_near_pair + slot, at(sib, dp))
+    for c in range(n_cut):
+        piece = out_ref.at[sib, rows_at(mine + starts[c], cuts[c]), :]
+        copies.arrived(piece, base_own + c, at(sib, dp))
+    rest = out_ref.at[sib, rows_at(theirs, half_rows), :]
+    copies.arrived(rest, base_own + n_cut, at(sib, dp))
+    for j in range(1, chips):
+        source = ((chip + chips - j) % chips) * 2 + (1 - core)
+        for c in range(n_cut):
+            slot = (j - 1) * n_cut + c
+            piece = out_ref.at[source, rows_at(mine + starts[c], cuts[c]), :]
+            copies.arrived(piece, base_near + slot, at(sib, dp))
+            piece = out_ref.at[source, rows_at(theirs + starts[c], cuts[c]), :]
+            copies.arrived(piece, base_near_pair + slot, at(sib, dp))
+    for j in range(1, n_group):
+        source = (me + n_group - j) % n_group
+        copies.arrived(gout_ref.at[source], base_gain + j - 1, at(source, dp))
+    copies.finish()
+
+
+def gather_weights(weights, gains, n_group, n_dp):
+    rows = weights.shape[0] // LANES
+    cuts = [units * TILE for units in cut_evenly(rows // 2 // TILE, 4)]
+    gain_size = gains.shape[0] * gains.shape[1]
+    gain_tile = (
+        jnp.zeros((TILE * LANES,), jnp.bfloat16)
+        .at[:gain_size]
+        .set(gains.astype(jnp.bfloat16).reshape(-1))
+        .reshape(TILE, LANES)
+    )
+    far = n_group // 2 - 1
+    slots = 4 * far * len(cuts) + len(cuts) + 1 + n_group - 1
+    vmem = pl.BlockSpec(memory_space=pltpu.VMEM)
+    full, full_gains = pl.pallas_call(
+        functools.partial(gather_kernel, n_group, n_dp, cuts),
+        out_shape=(
+            jax.ShapeDtypeStruct((n_group, rows, LANES), jnp.bfloat16),
+            jax.ShapeDtypeStruct((n_group, TILE, LANES), jnp.bfloat16),
+        ),
+        in_specs=[vmem, vmem],
+        out_specs=(vmem, vmem),
+        scratch_shapes=[pltpu.SemaphoreType.DMA((slots,)), pltpu.SemaphoreType.DMA((slots,))],
+        compiler_params=pltpu.CompilerParams(
+            collective_id=0, has_side_effects=True, vmem_limit_bytes=40 * 1024 * 1024
+        ),
+    )(weights.reshape(rows, LANES), gain_tile)
+    full_gains = full_gains.reshape(n_group, -1)[:, :gain_size]
+    full_gains = full_gains.reshape(n_group, gains.shape[0], gains.shape[1])
+    return full.reshape(-1), full_gains.transpose(1, 0, 2).reshape(gains.shape[0], -1)
+
+
+def reduce_kernel(
+    n_group, n_dp, cuts, main_rows, src_ref, tail_ref, out_ref,
+    buf1, buf2, sum2, buf3, sum3, buf4, send_sem, recv_sem,
+):
+    me, dp = lax.axis_index("group"), lax.axis_index("dp")
+    core, chip, chips = me % 2, me // 2, n_group // 2
+    sib = me + 1 - 2 * core
+    half = dp % 2
+    pair = dp + 1 - 2 * half
+    place, places = dp // 2, n_dp // 2
+    at = lambda rank, d: {"group": rank, "dp": d}
+    far_to = [((chip + j) % chips) * 2 + core for j in range(1, chips)]
+    line_to = [((place + j) % places) * 2 + half for j in range(1, places)]
+    greet(
+        [at(sib, dp)] + [at(rank, dp) for rank in far_to]
+        + [at(me, pair)] + [at(me, d) for d in line_to]
+    )
+    copies = Copies(send_sem, recv_sem)
+    per = 3 + (chips - 1) + 2 * (places - 1)
+    f32 = jnp.float32
+    starts = []
+    start = 0
+    for rows in cuts:
+        starts.append(start)
+        start += rows
+
+    def source(c):
+        if starts[c] < main_rows:
+            return src_ref, starts[c]
+        return tail_ref, starts[c] - main_rows
+
+    def send_core(c):
+        ref, off = source(c)
+        rows = cuts[c]
+        copies.start(
+            ref.at[:, 1 - core, pl.ds(off, rows), :],
+            buf1.at[:, pl.ds(starts[c], rows), :],
+            c * per,
+            at(sib, dp),
+        )
+
+    def after_core(c):
+        ref, off = source(c)
+        rows, o = cuts[c], starts[c]
+        copies.arrived(buf1.at[:, pl.ds(o, rows), :], c * per, at(sib, dp))
+        for j in range(1, chips):
+            k = (chip + j) % chips
+
+            def step(i, block):
+                here = rows_at(o + i, block)
+                total = buf1[k, here, :].astype(f32) + ref[
+                    k, core, rows_at(off + i, block), :
+                ].astype(f32)
+                buf1[k, here, :] = total.astype(jnp.bfloat16)
+
+            over_rows(rows, step)
+            copies.start(
+                buf1.at[k, pl.ds(o, rows), :],
+                buf2.at[j - 1, pl.ds(o, rows), :],
+                c * per + j,
+                at(far_to[j - 1], dp),
+            )
+
+    def after_far(c):
+        ref, off = source(c)
+        rows, o = cuts[c], starts[c]
+        for j in range(1, chips):
+            copies.arrived(buf2.at[j - 1, pl.ds(o, rows), :], c * per + j, at(far_to[j - 1], dp))
+
+        def step(i, block):
+            here = rows_at(o + i, block)
+            total = buf1[chip, here, :].astype(f32) + ref[
+                chip, core, rows_at(off + i, block), :
+            ].astype(f32)
+            for j in range(1, chips):
+                total = total + buf2[j - 1, here, :].astype(f32)
+            sum2[here, :] = total.astype(jnp.bfloat16)
+
+        over_rows(rows, step)
+        part = rows // 2
+        copies.start(
+            sum2.at[rows_at(o + (1 - half) * part, part), :],
+            buf3.at[pl.ds(o // 2, part), :],
+            c * per + chips,
+            at(me, pair),
+        )
+
+    def after_pair(c):
+        part, o = cuts[c] // 2, starts[c]
+        copies.arrived(buf3.at[pl.ds(o // 2, part), :], c * per + chips, at(me, pair))
+
+        def step(i, block):
+            here = rows_at(o // 2 + i, block)
+            total = sum2[rows_at(o + half * part + i, block), :].astype(f32)
+            sum3[here, :] = (total + buf3[here, :].astype(f32)).astype(jnp.bfloat16)
+
+        over_rows(part, step)
+        piece = part // places
+        for j in range(1, places):
+            to = (place + j) % places
+            copies.start(
+                sum3.at[rows_at(o // 2 + to * piece, piece), :],
+                buf4.at[j - 1, pl.ds(o // n_dp, piece), :],
+                c * per + chips + j,
+                at(me, line_to[j - 1]),
+            )
+
+    def after_line(c):
+        part, o = cuts[c] // 2, starts[c]
+        piece = part // places
+        for j in range(1, places):
+            copies.arrived(
+                buf4.at[j - 1, pl.ds(o // n_dp, piece), :],
+                c * per + chips + j,
+                at(me, line_to[j - 1]),
+            )
+        first = o + half * part + place * piece
+
+        def step(i, block):
+            total = sum3[rows_at(o // 2 + place * piece + i, block), :].astype(f32)
+            for j in range(1, places):
+                total = total + buf4[j - 1, rows_at(o // n_dp + i, block), :].astype(f32)
+            out_ref[rows_at(first + i, block), :] = total.astype(jnp.bfloat16)
+
+        over_rows(piece, step)
+        done = out_ref.at[rows_at(first, piece), :]
+        for j in range(1, places):
+            copies.start(done, done, c * per + chips + places - 1 + j, at(me, line_to[j - 1]))
+
+    def after_back(c):
+        part, o = cuts[c] // 2, starts[c]
+        piece = part // places
+        for j in range(1, places):
+            origin = (place + places - j) % places
+            copies.arrived(
+                out_ref.at[rows_at(o + half * part + origin * piece, piece), :],
+                c * per + chips + places - 1 + j,
+                at(me, line_to[j - 1]),
+            )
+        done = out_ref.at[rows_at(o + half * part, part), :]
+        copies.start(done, done, c * per + per - 1, at(me, pair))
+
+    def last(c):
+        part, o = cuts[c] // 2, starts[c]
+        copies.arrived(
+            out_ref.at[rows_at(o + (1 - half) * part, part), :], c * per + per - 1, at(me, pair)
+        )
+
+    n_cut = len(cuts)
+    for c in range(n_cut):
+        send_core(c)
+    stages = [after_core, after_far, after_pair, after_line, after_back, last]
+    lags = [0, 2, 3, 4, 5, 6]
+    for t in range(n_cut + lags[-1]):
+        for stage, lag in zip(stages, lags):
+            if 0 <= t - lag < n_cut:
+                stage(t - lag)
+    copies.finish()
+
+
+def reduce_grads(flat_grad, gain_grad, n_group, n_dp):
+    shard_rows = flat_grad.shape[0] // n_group // LANES
+    unit = TILE * n_dp
+    main_units = shard_rows // unit
+    main_rows = main_units * unit
+    spare = shard_rows - main_rows
+    gain_cols = gain_grad.shape[1] // n_group
+    gain_size = gain_grad.shape[0] * gain_cols
+    gain_flat = gain_grad.reshape(-1, n_group, gain_cols).transpose(1, 0, 2).reshape(n_group, -1)
+    gain_rows = -(-gain_size // LANES)
+    tail_rows = -(-(spare + gain_rows) // unit) * unit
+    gain_flat = jnp.pad(gain_flat, ((0, 0), (0, (tail_rows - spare) * LANES - gain_size)))
+    main = flat_grad.reshape(n_group, shard_rows, LANES)
+    tail = gain_flat.reshape(n_group, tail_rows - spare, LANES)
+    if spare:
+        tail = jnp.concatenate([main[:, main_rows:], tail], axis=1)
+    cuts = [units * unit for units in cut_evenly(main_units, 6)] + [tail_rows]
+    total_rows = main_rows + tail_rows
+    chips, places = n_group // 2, n_dp // 2
+    slots = len(cuts) * (3 + (chips - 1) + 2 * (places - 1))
+    vmem = pl.BlockSpec(memory_space=pltpu.VMEM)
+    bf16 = jnp.bfloat16
+    out = pl.pallas_call(
+        functools.partial(reduce_kernel, n_group, n_dp, cuts, main_rows),
+        out_shape=jax.ShapeDtypeStruct((total_rows, LANES), bf16),
+        in_specs=[vmem, vmem],
+        out_specs=vmem,
+        scratch_shapes=[
+            pltpu.VMEM((chips, total_rows, LANES), bf16),
+            pltpu.VMEM((chips - 1, total_rows, LANES), bf16),
+            pltpu.VMEM((total_rows, LANES), bf16),
+            pltpu.VMEM((total_rows // 2, LANES), bf16),
+            pltpu.VMEM((total_rows // 2, LANES), bf16),
+            pltpu.VMEM((places - 1, total_rows // n_dp, LANES), bf16),
+            pltpu.SemaphoreType.DMA((slots,)),
+            pltpu.SemaphoreType.DMA((slots,)),
+        ],
+        compiler_params=pltpu.CompilerParams(
+            collective_id=1, has_side_effects=True, vmem_limit_bytes=40 * 1024 * 1024
+        ),
+    )(
+        main.reshape(chips, 2, shard_rows, LANES),
+        tail.reshape(chips, 2, tail_rows, LANES),
+    )
+    grad_shard = out[:shard_rows].reshape(-1).astype(jnp.float32)
+    gain_shard = out[shard_rows : shard_rows + gain_rows].reshape(-1)[:gain_size]
+    return grad_shard, gain_shard.reshape(-1, gain_cols).astype(jnp.float32)
+
+
 def body(
+    n_group,
+    n_dp,
     hidden_in,
     out_grad,
     span_order,
@@ -168,10 +568,7 @@
     q_width = HEADS * HEAD_DIM
     kv_width = KV_HEADS * HEAD_DIM
     group_size = HEADS // KV_HEADS
-    full_flat, full_gains = (
-        lax.all_gather(weights.astype(jnp.bfloat16), "group", axis=0, tiled=True),
-        lax.all_gather(gains.astype(jnp.bfloat16), "group", axis=1, tiled=True),
-    )
+    full_flat, full_gains = gather_weights(weights, gains, n_group, n_dp)
     w_query, w_key, w_value, w_out, w_gate, w_up, w_down = split_weights(full_flat)
     gain_attn = full_gains[0].astype(jnp.float32)
     gain_ffn = full_gains[1].astype(jnp.float32)
@@ -281,15 +678,9 @@
         ]
     )
     gain_grad = jnp.stack([gg_attn, gg_ffn])
-    grad_part, gain_part = (
-        lax.psum_scatter(
-            flat_grad.astype(jnp.bfloat16), "group", scatter_dimension=0, tiled=True
-        ).astype(jnp.float32),
-        lax.psum_scatter(
-            gain_grad.astype(jnp.bfloat16), "group", scatter_dimension=1, tiled=True
-        ).astype(jnp.float32),
-    )
-    grad_shard, gain_shard = lax.psum((grad_part, gain_part), "dp")
+    grad_shard, gain_shard = reduce_grads(
+        flat_grad.astype(jnp.bfloat16), gain_grad.astype(jnp.bfloat16), n_group, n_dp
+    )
     new_weights, new_first, new_second = adamw_step(
         weights, first_moment, second_moment, grad_shard, DECAY_RATE, LEARN_RATE
     )
@@ -334,4 +725,6 @@
         P(None, "group"),
         P(None, "group"),
     )
-    return jax.shard_map(body, mesh=mesh, in_specs=in_specs, out_specs=out_specs, check_vma=False)
+    return jax.shard_map(
+        functools.partial(body, mesh.shape["group"], mesh.shape["dp"]),
+        mesh=mesh, in_specs=in_specs, out_specs=out_specs, check_vma=False)

time: 467 us -> 312 us (0.67)
  waiting for transfers between devices: 304 us -> 0.02 us
  Pallas kernels: 0 us -> 102 us
  local copies, waits for them, and re-layouts: 60.5 us -> 124 us
  blocking collectives: 34.4 us -> 7.04 us
  matrix products: 26.3 us -> 34.5 us
    unnamed x7 -> x1, waiting for transfers between devices: 137 us -> 0.02 us
    psum x1 -> x0, waiting for transfers between devices: 120 us -> none  [body(): grad_shard, gain_shard = lax.psum((grad_part, gain_part), 'dp')]
    pallas_call x0 -> x2, Pallas kernels: none -> 102 us  [the longest x1 70.8 us: reduce_grads(): pl.pallas_call(functools.partial(reduce_kernel, n_group, n_dp, cuts, main...]
    all_gather x1 -> x0, waiting for transfers between devices: 44.7 us -> none  [body(): lax.all_gather(weights.astype(jnp.bfloat16), 'group', axis=0, tiled=True)]
    psum x1 -> x0, blocking collectives: 21.9 us -> none  [body(): grad_shard, gain_shard = lax.psum((grad_part, gain_part), 'dp')]
    slice x10 -> x3, local copies, waits for them, and re-layouts: 20.9 us -> 29.6 us  [split_weights(): lax.slice_in_dim(flat_vector, offset, offset + amount, axis=0)]
    reshape x0 -> x7, local copies, waits for them, and re-layouts: none -> 8.55 us  [the longest x3 8.36 us: split_weights(): lax.slice_in_dim(flat_vector, offset, offset + amount, axis=0)]
    unnamed x159 -> x137, local copies, waits for them, and re-layouts: 13.3 us -> 20.3 us
  transfers between devices with their start and end apart: 5 -> 1, of which waited for: 5 -> 0; matrix products, arithmetic and copies ran while one was open for 9% -> 10% of each run, Pallas kernels for 0% -> 0%
where the time goes in v1:
time: 312 us; the launch traced here: 310 us
  local copies, waits for them, and re-layouts  124 us (40%)
  Pallas kernels  102 us (33%)
  matrix products  34.5 us (11%)
  other arithmetic  26.5 us (8%)
  between operations  15.1 us (5%)
  blocking collectives  7.04 us (2%)
    pallas_call x1, Pallas kernels, reduce_grads(): pl.pallas_call(functools.partial(reduce_kernel, n_group, n_dp, cuts, main...  70.8 us
    pallas_call x1, Pallas kernels, gather_weights(): pl.pallas_call(functools.partial(gather_kernel, n_group, n_dp, cuts), out...  31.7 us
    slice x3, local copies, waits for them, and re-layouts, split_weights(): lax.slice_in_dim(flat_vector, offset, offset + amount, axis=0)  29.6 us
    unnamed x137, local copies, waits for them, and re-layouts  20.3 us
    reshape x7, local copies, waits for them, and re-layouts, body(): grad_item.reshape(-1)  15 us
    sub x2, other arithmetic, adamw_step(): param_now - step_rate * (update + decay_weight * param_now)  8.93 us
    reshape x3, local copies, waits for them, and re-layouts, split_weights(): lax.slice_in_dim(flat_vector, offset, offset + amount, axis=0)  8.36 us
    all_gather x1, blocking collectives, body(): kv_all = lax.all_gather(kv_local, 'group', axis=1, tiled=True)  7.04 us
  transfers between devices with their start and end apart: 1, of which 0 were waited for; matrix products, arithmetic and copies ran while one was open for 10% of the time, Pallas kernels for 0%

profile of v1, /device:TPU:0, one launch (start us, length us, event | category | flops | bytes accessed | tf_op | source)
XLA Modules:
  0.0 309.6 jit_solution(4139138057771238452)
XLA Ops:
  8.5 2.0 copy-done.1
  10.5 31.7 %shard_map.168 = (bf16[4,6912,128]{2,1,0:T(8,128)(2,1)S(1)}, bf16[4,16,128]{2,1,0:T(8,128)(2,1)S(1)}) custom-call(f32[6912,128]{1,0:T(8,128)S(1)} %bitcast.202, bf16[16,128]{1,0:T(8,128)(2,1)S(1)} %pad_bitcast_fusion.1.g_ref), custom_call_target="tpu_custom_call" | custom-call | tf_op jit(solution)/shard_map/pallas_call | solution.py:324
  42.2 2.8 copy-done
  46.6 13.7 %slice.170 = bf16[6144,576]{1,0:T(8,128)(2,1)} reshape(bf16[4,6912,128]{2,1,0:T(8,128)(2,1)} %copy-done) | data formatting | bytes 14155776 | tf_op jit(solution)/shard_map/slice | solution.py:40
  60.3 14.4 %slice.160 = bf16[18432,192]{1,0:T(8,128)(2,1)} reshape(bf16[4,6912,128]{2,1,0:T(8,128)(2,1)} %copy-done) | data formatting | bytes 14155776 | tf_op jit(solution)/shard_map/slice | solution.py:40
  93.7 1.7 copy.110
  98.1 2.8 reshape.484
  100.8 2.0 reshape.483
  102.9 3.6 %reshape.482 = bf16[576,1536]{1,0:T(8,128)(2,1)S(1)} reshape(bf16[1,6912,128]{2,1,0:T(8,128)(2,1)} %get-tuple-element.53) | data formatting | bytes 3538944 | tf_op jit(solution)/shard_map/reshape | solution.py:40
  106.5 2.0 slice_bitcast_fusion
  108.6 2.3 copy.103
  112.5 2.0 convolution_convert_fusion.10
  117.7 1.8 copy.94
  125.5 1.9 pad_maximum_fusion.2
  127.4 1.7 copy.99
  129.1 7.0 %all_gather.4 = bf16[2,256,384]{2,0,1:T(2,128)(2,1)S(1)} all-gather(bf16[2,64,384]{2,0,1:T(2,128)(2,1)} %copy.99), channel_id=1, replica_groups=mesh['dp'=8,'group'=4] {'group'}, dimensions={1}, use_global_device_ids=true | all-gather | bytes 491520 | tf_op jit(solution)/shard_map/all_gather | solution.py:593
  141.5 1.7 fusion.44
  153.3 1.8 multiply_reduce_fusion.5
  172.4 2.1 constant_dynamic-update-slice_fusion.6
  174.5 1.8 convolution_add_fusion.2
  179.3 1.8 convolution_convert_fusion.1
  181.2 3.2 %reshape.500 = bf16[884736]{0:T(1024)(128)(2,1)} reshape(bf16[576,1536]{1,0:T(8,128)(2,1)S(1)} %convolution_convert_fusion.1) | data formatting | bytes 3538944 | tf_op jit(solution)/shard_map/reshape | solution.py:676
  185.0 3.2 %reshape.499 = bf16[884736]{0:T(1024)(128)(2,1)} reshape(bf16[576,1536]{1,0:T(8,128)(2,1)S(1)} %convolution_convert_fusion.2) | data formatting | bytes 3538944 | tf_op jit(solution)/shard_map/reshape | solution.py:676
  188.2 1.9 convolution_convert_fusion
  190.1 2.8 copy.124
  192.9 3.2 %reshape.501 = bf16[884736]{0:T(1024)(128)(2,1)} reshape(bf16[1536,576]{1,0:T(8,128)(2,1)S(1)} %copy.124) | data formatting | bytes 3538944 | tf_op jit(solution)/shard_map/reshape | solution.py:676
  196.1 2.3 fusion.16
  207.2 2.0 copy.121
  212.6 2.0 constant_dynamic-update-slice_fusion.3
  218.6 3.0 copy-done.3
  221.7 70.8 %shard_map.169 = bf16[7040,128]{1,0:T(8,128)(2,1)S(1)} custom-call(bf16[2,2,6912,128]{3,2,1,0:T(8,128)(2,1)S(1)} %bitcast.203, bf16[2,2,128,128]{3,2,1,0:T(8,128)(2,1)S(1)} %bitcast.204), custom_call_target="tpu_custom_call" | custom-call | tf_op jit(solution)/shard_map/pallas_call | solution.py:524
  293.8 8.3 %multiply_subtract_fusion = (f32[884736]{0:T(1024)}, f32[884736]{0:T(1024)}, f32[884736]{0:T(1024)}, f32[884736]{0:T(1024)}) fusion(f32[884736]{0:T(1024)S(1)} %copy-done.2, f32[884736]{0:T(1024)} %param.15, f32[884736]{0:T(1024)} %param.16, bf16[7040,128]{1,0:T(8,128)(2,1)} %copy-done.4), kind=kLoop, calls=%fused_computation.2 | loop fusion | flops 14155776 | bytes 26542080 | tf_op jit(solution)/shard_map/sub | solution.py:96
  (251 shorter events, 89.1 us)
Async XLA Ops:
  7.2 191.2 %reduce-scatter.2.cloned.1.call-start = ((), (), s32[]{:S(2)}) async-start(), calls=%async_computation.1 | async-start | bytes 983040 | tf_op jit(solution)/shard_map/reduce_scatter | solution.py:652
  102.9 9.6 %copy-start.48 = (f32[576]{0:T(1024)S(1)}, f32[576]{0:T(1024)}, u32[]{:S(2)}) copy-start(f32[576]{0:T(1024)} %copy-done.47) | copy-start | bytes 6916
  102.9 9.6 %copy-start.55 = (f32[128]{0:T(128)S(1)}, f32[128]{0:T(128)}, u32[]{:S(2)}) copy-start(f32[128]{0:T(128)} %rsqrt.21) | copy-start | bytes 1540
  106.5 15.8 %copy-start.62 = (f32[32]{0:T(128)S(1)}, f32[32]{0:T(128)}, u32[]{:S(2)}) copy-start(f32[32]{0:T(128)} %multiply_power_fusion) | copy-start | bytes 388
  106.5 15.8 %copy-start.63 = (f32[128]{0:T(128)S(1)}, f32[128]{0:T(128)}, u32[]{:S(2)}) copy-start(f32[128]{0:T(128)} %convert_element_type.181) | copy-start | bytes 1540
  122.5 25.2 %copy-start.57 = (s32[256]{0:T(256)S(1)}, s32[256]{0:T(256)}, u32[]{:S(2)}) copy-start(s32[256]{0:T(256)} %le.56) | copy-start | bytes 3076
  122.5 25.2 %copy-start.58 = (s32[256]{0:T(256)S(1)}, s32[256]{0:T(256)}, u32[]{:S(2)}) copy-start(s32[256]{0:T(256)} %le.61) | copy-start | bytes 3076
  122.5 25.2 %copy-start.59 = (s32[64]{0:T(128)S(1)}, s32[64]{0:T(128)}, u32[]{:S(2)}) copy-start(s32[64]{0:T(128)} %get-tuple-element.77) | copy-start | bytes 772
  144.9 10.3 %copy-start.51 = (f32[576]{0:T(1024)S(1)}, f32[576]{0:T(1024)}, u32[]{:S(2)}) copy-start(f32[576]{0:T(1024)} %reshape.506) | copy-start | bytes 6916
  146.6 6.4 %copy-start.31 = (bf16[256,192]{0,1:T(8,128)(2,1)S(1)}, bf16[256,192]{0,1:T(8,128)(2,1)}, u32[]{:S(2)}) copy-start(bf16[256,192]{0,1:T(8,128)(2,1)} %copy.107) | copy-start | bytes 294916
  146.6 6.7 %copy-start.7 = (f32[128,576]{0,1:T(8,128)S(1)}, f32[128,576]{0,1:T(8,128)}, u32[]{:S(2)}) copy-start(f32[128,576]{0,1:T(8,128)} %copy.110) | copy-start | bytes 884740
  151.7 11.5 %copy-start.50 = (f32[3,3,64]{2,1,0:T(4,128)}, f32[3,3,64]{2,1,0:T(4,128)S(1)}, u32[]{:S(2)}) copy-start(f32[3,3,64]{2,1,0:T(4,128)S(1)} %log_add_fusion) | copy-start | bytes 6916
  152.9 9.1 %copy-start.21 = (bf16[3,64,3,64]{3,1,2,0:T(8,128)(2,1)}, bf16[3,64,3,64]{3,1,2,0:T(8,128)(2,1)S(1)}, u32[]{:S(2)}) copy-start(bf16[3,64,3,64]{3,1,2,0:T(8,128)(2,1)S(1)} %convolution_convert_fusion.9) | copy-start | bytes 221188
  153.3 8.7 %copy-start.23 = (bf16[3,64,3,64]{3,1,2,0:T(8,128)(2,1)}, bf16[3,64,3,64]{3,1,2,0:T(8,128)(2,1)S(1)}, u32[]{:S(2)}) copy-start(bf16[3,64,3,64]{3,1,2,0:T(8,128)(2,1)S(1)} %convolution_convert_fusion.8) | copy-start | bytes 221188
  160.2 17.0 %copy-start.19 = (f32[128,576]{0,1:T(8,128)}, f32[128,576]{0,1:T(8,128)S(1)}, u32[]{:S(2)}) copy-start(f32[128,576]{0,1:T(8,128)S(1)} %multiply_add_fusion.2) | copy-start | bytes 884740
  166.4 8.1 %copy-start.10 = (bf16[1536,576]{1,0:T(8,128)(2,1)S(1)}, bf16[1536,576]{1,0:T(8,128)(2,1)}, u32[]{:S(2)}) copy-start(bf16[1536,576]{1,0:T(8,128)(2,1)} %reshape.484) | copy-start | bytes 5308420
  166.4 8.1 %copy-start.12 = (f32[128,576]{0,1:T(8,128)S(1)}, f32[128,576]{0,1:T(8,128)}, u32[]{:S(2)}) copy-start(f32[128,576]{0,1:T(8,128)} %copy-done.11) | copy-start | bytes 884740
  172.4 6.9 %copy-start.18 = (bf16[128,576]{0,1:T(8,128)(2,1)S(1)}, bf16[128,576]{0,1:T(8,128)(2,1)}, u32[]{:S(2)}) copy-start(bf16[128,576]{0,1:T(8,128)(2,1)} %copy-done.17) | copy-start | bytes 442372
  177.6 6.7 %copy-start.26 = (bf16[128,1536]{1,0:T(8,128)(2,1)S(1)}, bf16[128,1536]{1,0:T(8,128)(2,1)}, u32[]{:S(2)}) copy-start(bf16[128,1536]{1,0:T(8,128)(2,1)} %copy-done.25) | copy-start | bytes 1179652
  192.8 6.4 %copy-start.8 = (f32[128,576]{0,1:T(8,128)S(1)}, f32[128,576]{0,1:T(8,128)}, u32[]{:S(2)}) copy-start(f32[128,576]{0,1:T(8,128)} %copy.110) | copy-start | bytes 884740
  192.9 6.4 %copy-start.49 = (f32[576]{0:T(1024)S(1)}, f32[576]{0:T(1024)}, u32[]{:S(2)}) copy-start(f32[576]{0:T(1024)} %copy-done.47) | copy-start | bytes 6916
  192.9 6.4 %copy-start.56 = (f32[128]{0:T(128)S(1)}, f32[128]{0:T(128)}, u32[]{:S(2)}) copy-start(f32[128]{0:T(128)} %rsqrt.21) | copy-start | bytes 1540
  192.9 9.2 %copy-start.43 = (f32[128,32]{0,1:T(8,128)S(1)}, f32[128,32]{0,1:T(8,128)}, u32[]{:S(2)}) copy-start(f32[128,32]{0,1:T(8,128)} %copy-done.41) | copy-start | bytes 49156
  192.9 9.2 %copy-start.46 = (f32[128,32]{0,1:T(8,128)S(1)}, f32[128,32]{0,1:T(8,128)}, u32[]{:S(2)}) copy-start(f32[128,32]{0,1:T(8,128)} %copy-done.44) | copy-start | bytes 49156
  196.1 10.3 %copy-start.20 = (f32[128,576]{0,1:T(8,128)S(1)}, f32[128,576]{0,1:T(8,128)}, u32[]{:S(2)}) copy-start(f32[128,576]{0,1:T(8,128)} %copy-done.19) | copy-start | bytes 884740
  203.5 11.0 %copy-start.15 = (bf16[884736]{0:T(1024)(128)(2,1)S(1)}, bf16[884736]{0:T(1024)(128)(2,1)}, u32[]{:S(2)}) copy-start(bf16[884736]{0:T(1024)(128)(2,1)} %reshape.499) | copy-start | bytes 5308420
  207.2 8.7 %copy-start.14 = (bf16[884736]{0:T(1024)(128)(2,1)S(1)}, bf16[884736]{0:T(1024)(128)(2,1)}, u32[]{:S(2)}) copy-start(bf16[884736]{0:T(1024)(128)(2,1)} %reshape.500) | copy-start | bytes 5308420
  221.7 72.2 %copy-start.2 = (f32[884736]{0:T(1024)S(1)}, f32[884736]{0:T(1024)}, u32[]{:S(2)}) copy-start(f32[884736]{0:T(1024)} %param.14) | copy-start | bytes 10616836
  293.8 8.4 %copy-start.54 = (f32[2,144]{1,0:T(2,128)}, f32[2,144]{1,0:T(2,128)S(1)}, u32[]{:S(2)}) copy-start(f32[2,144]{1,0:T(2,128)S(1)} %reshape.508) | copy-start | bytes 3460
  293.8 8.4 %copy-start.53 = (f32[2,144]{1,0:T(2,128)S(1)}, f32[2,144]{1,0:T(2,128)}, u32[]{:S(2)}) copy-start(f32[2,144]{1,0:T(2,128)} %param.17) | copy-start | bytes 3460
  293.8 8.4 %copy-start.60 = (f32[2,144]{1,0:T(2,128)S(1)}, f32[2,144]{1,0:T(2,128)}, u32[]{:S(2)}) copy-start(f32[2,144]{1,0:T(2,128)} %param.18) | copy-start | bytes 3460
  293.8 8.4 %copy-start.61 = (f32[2,144]{1,0:T(2,128)S(1)}, f32[2,144]{1,0:T(2,128)}, u32[]{:S(2)}) copy-start(f32[2,144]{1,0:T(2,128)} %param.19) | copy-start | bytes 3460
  (33 other events, 107.1 us)
Sparse Core Ops, SparseCore 0:
  166.5 23.6 reduce-scatter.1

commit v2 on v1

--- a/solution.py
+++ b/solution.py
@@ -26,6 +26,8 @@
 CORRECT_ONE = 1.0 - 0.9**5
 CORRECT_TWO = 1.0 - 0.95**5
 NEG_LARGE = -1e30
+LANES = 128
+TILE = 16
 
 
 def split_weights(flat_vector):
@@ -36,9 +38,10 @@
     offset = 0
     for rows_cols in layout:
         amount = rows_cols[0] * rows_cols[1]
-        pieces.append(
-            lax.slice_in_dim(flat_vector, offset, offset + amount, axis=0).reshape(rows_cols)
-        )
+        piece = lax.slice_in_dim(
+            flat_vector, offset // LANES, (offset + amount) // LANES, axis=0
+        )
+        pieces.append(lax.optimization_barrier(piece).reshape(rows_cols))
         offset = offset + amount
     return pieces
 
@@ -152,10 +155,6 @@
         [grad_key.reshape(key_rows, -1), grad_value.reshape(key_rows, -1)], axis=-1
     )
     return (grad_query, stacked)
-
-
-LANES = 128
-TILE = 16
 
 
 def cut_evenly(total_units, most):
@@ -331,18 +330,19 @@
         out_specs=(vmem, vmem),
         scratch_shapes=[pltpu.SemaphoreType.DMA((slots,)), pltpu.SemaphoreType.DMA((slots,))],
         compiler_params=pltpu.CompilerParams(
-            collective_id=0, has_side_effects=True, vmem_limit_bytes=40 * 1024 * 1024
+            collective_id=0, has_side_effects=True, vmem_limit_bytes=16 * 1024 * 1024
         ),
     )(weights.reshape(rows, LANES), gain_tile)
     full_gains = full_gains.reshape(n_group, -1)[:, :gain_size]
     full_gains = full_gains.reshape(n_group, gains.shape[0], gains.shape[1])
-    return full.reshape(-1), full_gains.transpose(1, 0, 2).reshape(gains.shape[0], -1)
-
-
-def reduce_kernel(
-    n_group, n_dp, cuts, main_rows, src_ref, tail_ref, out_ref,
-    buf1, buf2, sum2, buf3, sum3, buf4, send_sem, recv_sem,
-):
+    return full.reshape(-1, LANES), full_gains.transpose(1, 0, 2).reshape(gains.shape[0], -1)
+
+
+def reduce_kernel(n_group, n_dp, cuts, moves, *refs):
+    pieces = refs[: 1 + max(move[0] for move in moves)]
+    (gain_ref, out_ref, src, buf1, buf2, sum2, buf3, sum3, buf4, send_sem, recv_sem, local_sem) = refs[
+        len(pieces) :
+    ]
     me, dp = lax.axis_index("group"), lax.axis_index("dp")
     core, chip, chips = me % 2, me // 2, n_group // 2
     sib = me + 1 - 2 * core
@@ -352,6 +352,25 @@
     at = lambda rank, d: {"group": rank, "dp": d}
     far_to = [((chip + j) % chips) * 2 + core for j in range(1, chips)]
     line_to = [((place + j) % places) * 2 + half for j in range(1, places)]
+    local = []
+    for number, (piece, first, rank, row, rows) in enumerate(moves):
+        local.append(
+            pltpu.make_async_copy(
+                pieces[piece].at[pl.ds(first, rows), :],
+                src.at[rank // 2, rank % 2, pl.ds(row, rows), :],
+                local_sem.at[number],
+            )
+        )
+    gain_rows = gain_ref.shape[2]
+    local.append(
+        pltpu.make_async_copy(
+            gain_ref,
+            src.at[:, :, pl.ds(src.shape[2] - gain_rows, gain_rows), :],
+            local_sem.at[len(moves)],
+        )
+    )
+    for copy in local:
+        copy.start()
     greet(
         [at(sib, dp)] + [at(rank, dp) for rank in far_to]
         + [at(me, pair)] + [at(me, d) for d in line_to]
@@ -359,29 +378,21 @@
     copies = Copies(send_sem, recv_sem)
     per = 3 + (chips - 1) + 2 * (places - 1)
     f32 = jnp.float32
-    starts = []
-    start = 0
-    for rows in cuts:
-        starts.append(start)
-        start += rows
-
-    def source(c):
-        if starts[c] < main_rows:
-            return src_ref, starts[c]
-        return tail_ref, starts[c] - main_rows
+    starts = [start for start, _ in cuts]
+    cuts = [rows for _, rows in cuts]
+    for copy in local:
+        copy.wait()
 
     def send_core(c):
-        ref, off = source(c)
         rows = cuts[c]
         copies.start(
-            ref.at[:, 1 - core, pl.ds(off, rows), :],
+            src.at[:, 1 - core, pl.ds(starts[c], rows), :],
             buf1.at[:, pl.ds(starts[c], rows), :],
             c * per,
             at(sib, dp),
         )
 
     def after_core(c):
-        ref, off = source(c)
         rows, o = cuts[c], starts[c]
         copies.arrived(buf1.at[:, pl.ds(o, rows), :], c * per, at(sib, dp))
         for j in range(1, chips):
@@ -389,9 +400,7 @@
 
             def step(i, block):
                 here = rows_at(o + i, block)
-                total = buf1[k, here, :].astype(f32) + ref[
-                    k, core, rows_at(off + i, block), :
-                ].astype(f32)
+                total = buf1[k, here, :].astype(f32) + src[k, core, here, :].astype(f32)
                 buf1[k, here, :] = total.astype(jnp.bfloat16)
 
             over_rows(rows, step)
@@ -403,16 +412,13 @@
             )
 
     def after_far(c):
-        ref, off = source(c)
         rows, o = cuts[c], starts[c]
         for j in range(1, chips):
             copies.arrived(buf2.at[j - 1, pl.ds(o, rows), :], c * per + j, at(far_to[j - 1], dp))
 
         def step(i, block):
             here = rows_at(o + i, block)
-            total = buf1[chip, here, :].astype(f32) + ref[
-                chip, core, rows_at(off + i, block), :
-            ].astype(f32)
+            total = buf1[chip, here, :].astype(f32) + src[chip, core, here, :].astype(f32)
             for j in range(1, chips):
                 total = total + buf2[j - 1, here, :].astype(f32)
             sum2[here, :] = total.astype(jnp.bfloat16)
@@ -499,8 +505,19 @@
     copies.finish()
 
 
-def reduce_grads(flat_grad, gain_grad, n_group, n_dp):
-    shard_rows = flat_grad.shape[0] // n_group // LANES
+def taper(total_units):
+    cap = -(-total_units // 6)
+    sizes = []
+    while total_units:
+        size = min(total_units, max(3, min(cap, total_units // 3)))
+        sizes.append(size)
+        total_units -= size
+    return sizes
+
+
+def reduce_grads(weight_parts, gain_grad, n_group, n_dp):
+    pieces = [part.astype(jnp.bfloat16).reshape(-1, LANES) for part in weight_parts]
+    shard_rows = sum(piece.shape[0] for piece in pieces) // n_group
     unit = TILE * n_dp
     main_units = shard_rows // unit
     main_rows = main_units * unit
@@ -511,22 +528,34 @@
     gain_rows = -(-gain_size // LANES)
     tail_rows = -(-(spare + gain_rows) // unit) * unit
     gain_flat = jnp.pad(gain_flat, ((0, 0), (0, (tail_rows - spare) * LANES - gain_size)))
-    main = flat_grad.reshape(n_group, shard_rows, LANES)
-    tail = gain_flat.reshape(n_group, tail_rows - spare, LANES)
-    if spare:
-        tail = jnp.concatenate([main[:, main_rows:], tail], axis=1)
-    cuts = [units * unit for units in cut_evenly(main_units, 6)] + [tail_rows]
     total_rows = main_rows + tail_rows
     chips, places = n_group // 2, n_dp // 2
+    cuts = [(main_rows, tail_rows)]
+    start = 0
+    for size in taper(main_units):
+        cuts.append((start, size * unit))
+        start += size * unit
+    moves = []
+    begin = 0
+    for number, piece in enumerate(pieces):
+        first, end = begin, begin + piece.shape[0]
+        while first < end:
+            rank = first // shard_rows
+            stop = min(end, (rank + 1) * shard_rows)
+            moves.append((number, first - begin, rank, first - rank * shard_rows, stop - first))
+            first = stop
+        begin = end
     slots = len(cuts) * (3 + (chips - 1) + 2 * (places - 1))
     vmem = pl.BlockSpec(memory_space=pltpu.VMEM)
+    anywhere = pl.BlockSpec(memory_space=pl.ANY)
     bf16 = jnp.bfloat16
     out = pl.pallas_call(
-        functools.partial(reduce_kernel, n_group, n_dp, cuts, main_rows),
+        functools.partial(reduce_kernel, n_group, n_dp, cuts, moves),
         out_shape=jax.ShapeDtypeStruct((total_rows, LANES), bf16),
-        in_specs=[vmem, vmem],
+        in_specs=[anywhere] * (len(pieces) + 1),
         out_specs=vmem,
         scratch_shapes=[
+            pltpu.VMEM((chips, 2, total_rows, LANES), bf16),
             pltpu.VMEM((chips, total_rows, LANES), bf16),
             pltpu.VMEM((chips - 1, total_rows, LANES), bf16),
             pltpu.VMEM((total_rows, LANES), bf16),
@@ -535,14 +564,12 @@
             pltpu.VMEM((places - 1, total_rows // n_dp, LANES), bf16),
             pltpu.SemaphoreType.DMA((slots,)),
             pltpu.SemaphoreType.DMA((slots,)),
+            pltpu.SemaphoreType.DMA((len(moves) + 1,)),
         ],
         compiler_params=pltpu.CompilerParams(
-            collective_id=1, has_side_effects=True, vmem_limit_bytes=40 * 1024 * 1024
+            collective_id=1, has_side_effects=True, vmem_limit_bytes=22 * 1024 * 1024
         ),
-    )(
-        main.reshape(chips, 2, shard_rows, LANES),
-        tail.reshape(chips, 2, tail_rows, LANES),
-    )
+    )(*pieces, gain_flat.reshape(chips, 2, tail_rows - spare, LANES))
     grad_shard = out[:shard_rows].reshape(-1).astype(jnp.float32)
     gain_shard = out[shard_rows : shard_rows + gain_rows].reshape(-1)[:gain_size]
     return grad_shard, gain_shard.reshape(-1, gain_cols).astype(jnp.float32)
@@ -671,15 +698,12 @@
     )
     gg_attn = jnp.sum(grad_attn_in * normed_one, axis=0)
     in_grad = grad_middle + norm_backward(grad_attn_in * gain_attn, normed_one, factor_one)
-    flat_grad = jnp.concatenate(
-        [
-            grad_item.reshape(-1)
-            for grad_item in (gw_query, gw_key, gw_value, gw_out, gw_gate, gw_up, gw_down)
-        ]
-    )
     gain_grad = jnp.stack([gg_attn, gg_ffn])
     grad_shard, gain_shard = reduce_grads(
-        flat_grad.astype(jnp.bfloat16), gain_grad.astype(jnp.bfloat16), n_group, n_dp
+        (gw_query, gw_key, gw_value, gw_out, gw_gate, gw_up, gw_down),
+        gain_grad.astype(jnp.bfloat16),
+        n_group,
+        n_dp,
     )
     new_weights, new_first, new_second = adamw_step(
         weights, first_moment, second_moment, grad_shard, DECAY_RATE, LEARN_RATE

time: 312 us -> 232 us (0.74)
  local copies, waits for them, and re-layouts: 124 us -> 56.9 us
  other arithmetic: 26.5 us -> 16 us
  Pallas kernels: 102 us -> 110 us
  matrix products: 34.5 us -> 26.8 us
    slice x3, local copies, waits for them, and re-layouts: 29.6 us -> 2.61 us  [split_weights(): lax.slice_in_dim(flat_vector, offset // LANES, (offset + amount) // LANES...]
    pallas_call x1, Pallas kernels: 70.8 us -> 77.9 us  [reduce_grads(): pl.pallas_call(functools.partial(reduce_kernel, n_group, n_dp, cuts, move...]
    unnamed x137 -> x147, local copies, waits for them, and re-layouts: 20.3 us -> 13.7 us
    slice x4, local copies, waits for them, and re-layouts: 5.78 us -> 0.41 us  [split_pair(): key_blk = kv_seq[:, :kv_width].reshape(-1, KV_HEADS, HEAD_DIM)]
    add x4, local copies, waits for them, and re-layouts: 4.62 us -> 0.23 us  [body(): span_order[:, :, None] * SPAN + offsets[None, None, :]]
    reshape x10 -> x14, local copies, waits for them, and re-layouts: 23.4 us -> 27.6 us  [the longest x7 14.6 us: reduce_grads(): part.astype(jnp.bfloat16).reshape(-1, LANES)]
    dot_general x2 -> x1, local copies, waits for them, and re-layouts: 4.31 us -> 0.36 us  [body(): jnp.dot(attn_in, w_query, preferred_element_type=jnp.float32)]
    le x3, local copies, waits for them, and re-layouts: 3.97 us -> 0.16 us  [masked_scores(): allowed = key_pos[None, :] <= query_pos[:, None]]
  transfers between devices with their start and end apart: 1 -> 1, of which waited for: 0 -> 0; matrix products, arithmetic and copies ran while one was open for 10% -> 13% of each run, Pallas kernels for 0% -> 0%
where the time goes in v2:
time: 232 us; the launch traced here: 231 us
  Pallas kernels  110 us (47%)
  local copies, waits for them, and re-layouts  56.9 us (25%)
  matrix products  26.8 us (12%)
  other arithmetic  16 us (7%)
  between operations  15.3 us (7%)
  blocking collectives  6.67 us (3%)
    pallas_call x1, Pallas kernels, reduce_grads(): pl.pallas_call(functools.partial(reduce_kernel, n_group, n_dp, cuts, move...  77.9 us
    pallas_call x1, Pallas kernels, gather_weights(): pl.pallas_call(functools.partial(gather_kernel, n_group, n_dp, cuts), out...  31.7 us
    reshape x7, local copies, waits for them, and re-layouts, reduce_grads(): part.astype(jnp.bfloat16).reshape(-1, LANES)  14.6 us
    unnamed x147, local copies, waits for them, and re-layouts  13.7 us
    reshape x7, local copies, waits for them, and re-layouts, split_weights(): pieces.append(lax.optimization_barrier(piece).reshape(rows_cols))  13 us
    sub x2, other arithmetic, adamw_step(): param_now - step_rate * (update + decay_weight * param_now)  8.93 us
    all_gather x1, blocking collectives, body(): kv_all = lax.all_gather(kv_local, 'group', axis=1, tiled=True)  6.67 us
    dot_general x7, matrix products, outer_sum(): lax.dot_general(left_rows, right_rows, (((0,), (0,)), ((), ())), preferre...  5.43 us
  transfers between devices with their start and end apart: 1, of which 0 were waited for; matrix products, arithmetic and copies ran while one was open for 13% of the time, Pallas kernels for 0%

profile of v2, /device:TPU:0, one launch (start us, length us, event | category | flops | bytes accessed | tf_op | source)
XLA Modules:
  0.0 231.3 jit_solution(16325431978870140729)
XLA Ops:
  8.0 2.0 copy-done
  10.0 31.7 %shard_map.168 = (bf16[4,6912,128]{2,1,0:T(8,128)(2,1)S(1)}, bf16[4,16,128]{2,1,0:T(8,128)(2,1)S(1)}) custom-call(f32[6912,128]{1,0:T(8,128)S(1)} %bitcast.213, bf16[16,128]{1,0:T(8,128)(2,1)S(1)} %pad_bitcast_fusion.1.g_ref), custom_call_target="tpu_custom_call" | custom-call | tf_op jit(solution)/shard_map/pallas_call | solution.py:323
  41.9 2.5 %slice_bitcast_fusion = (bf16[6912,128]{1,0:T(8,128)(2,1)}, bf16[6912,128]{1,0:T(8,128)(2,1)}, bf16[6912,128]{1,0:T(8,128)(2,1)}) fusion(bf16[4,6912,128]{2,1,0:T(8,128)(2,1)S(1)} %get-tuple-element.25), kind=kLoop, calls=%fused_computation.9 | loop fusion | bytes 10616832 | tf_op jit(solution)/shard_map/slice | solution.py:41
  48.4 6.7 %all_gather.4 = bf16[2,256,384]{2,0,1:T(2,128)(2,1)S(1)} all-gather(bf16[2,64,384]{2,0,1:T(2,128)(2,1)S(1)} %copy.101), channel_id=1, replica_groups=mesh['dp'=8,'group'=4] {'group'}, dimensions={1}, use_global_device_ids=true | all-gather | bytes 491520 | tf_op jit(solution)/shard_map/all_gather | solution.py:620
  61.0 1.3 multiply_reduce_fusion.5
  62.8 3.6 %reshape.497 = bf16[576,1536]{1,0:T(8,128)(2,1)S(1)} reshape(bf16[6912,128]{1,0:T(8,128)(2,1)} %get-tuple-element.53) | data formatting | bytes 3538944 | tf_op jit(solution)/shard_map/reshape | solution.py:44
  66.4 3.6 %reshape.498 = bf16[576,1536]{1,0:T(8,128)(2,1)S(1)} reshape(bf16[6912,128]{1,0:T(8,128)(2,1)} %get-tuple-element.52) | data formatting | bytes 3538944 | tf_op jit(solution)/shard_map/reshape | solution.py:44
  71.1 1.4 fusion.48
  72.5 1.4 fusion.49
  73.9 4.3 %reshape.499 = bf16[1536,576]{1,0:T(8,128)(2,1)} reshape(bf16[6912,128]{1,0:T(8,128)(2,1)} %get-tuple-element.51) | data formatting | bytes 3538944 | tf_op jit(solution)/shard_map/reshape | solution.py:44
  78.1 1.7 copy.114
  79.8 3.6 %multiply_convert_fusion = (bf16[128,1536]{1,0:T(8,128)(2,1)S(1)}, bf16[128,1536]{1,0:T(8,128)(2,1)S(1)}, bf16[128,1536]{1,0:T(8,128)(2,1)}) fusion(f32[128,1536]{1,0:T(8,128)} %fusion.48, f32[128,1536]{1,0:T(8,128)} %fusion.49, bf16[1536,576]{1,0:T(8,128)(2,1)} %reshape.499, bf16[128,576]{1,0:T(8,128)(2,1)} %bitcast.261), kind=kOutput, calls=%fused_computation.44 | convolution fusion | flops 229638144 | bytes 4669440 | tf_op jit(solution)/shard_map/dot_general | solution.py:641
  84.6 1.3 multiply_reduce_fusion.1
  92.3 1.9 convolution_bitcast_fusion.4
  94.2 1.8 convolution_add_fusion.2
  96.9 1.2 pad_maximum_fusion.1
  99.3 1.6 reshape.510.refs_0_
  101.3 1.6 reshape.513.refs_3_
  102.9 1.6 convolution_convert_fusion.2
  104.5 3.2 %reshape.514.refs_4_ = bf16[6912,128]{1,0:T(8,128)(2,1)} reshape(bf16[576,1536]{1,0:T(8,128)(2,1)S(1)} %convolution_convert_fusion.2) | data formatting | bytes 3538944 | tf_op jit(solution)/shard_map/reshape | solution.py:519
  108.4 3.0 %reshape.515.refs_5_ = bf16[6912,128]{1,0:T(8,128)(2,1)} reshape(bf16[576,1536]{1,0:T(8,128)(2,1)S(1)} %convolution_convert_fusion.1) | data formatting | bytes 3538944 | tf_op jit(solution)/shard_map/reshape | solution.py:519
  111.4 1.9 convolution_convert_fusion
  113.3 2.7 %copy.127 = bf16[1536,576]{1,0:T(8,128)(2,1)S(1)} copy(bf16[1536,576]{0,1:T(8,128)(2,1)} %convolution_convert_fusion) | data formatting | bytes 3538944 | tf_op jit(solution)/shard_map/convert_element_type | solution.py:519
  116.1 3.0 %reshape.516.refs_6_ = bf16[6912,128]{1,0:T(8,128)(2,1)} reshape(bf16[1536,576]{1,0:T(8,128)(2,1)S(1)} %copy.127) | data formatting | bytes 3538944 | tf_op jit(solution)/shard_map/reshape | solution.py:519
  119.2 1.3 fusion.53
  120.6 1.3 fusion.28
  127.7 1.5 copy-done.3
  129.2 1.5 copy-done.4
  130.7 1.5 copy-done.5
  136.2 77.9 %shard_map.169 = bf16[7040,128]{1,0:T(8,128)(2,1)S(1)} custom-call(bf16[2592,128]{1,0:T(8,128)(2,1)S(1)} %copy-done.6, bf16[864,128]{1,0:T(8,128)(2,1)S(1)} %copy-done.8, bf16[864,128]{1,0:T(8,128)(2,1)S(1)} %copy-done.9, bf16[2592,128]{1,0:T(8,128)(2,1)S(1)} %copy-done.7, bf16[6912,128]{1,0:T(8,128)(2,1)S(1)} %copy-done.4, bf16[6912,128]{1,0:T(8,128)(2,1)S(1)} %copy-done.5, ...), custom_call_target="tpu_custom_call" | custom-call | tf_op jit(solution)/shard_map/pallas_call | solution.py:552
  214.1 1.3 copy-done.2
  215.5 8.3 %multiply_subtract_fusion = (f32[884736]{0:T(1024)}, f32[884736]{0:T(1024)}, f32[884736]{0:T(1024)}, f32[884736]{0:T(1024)}) fusion(f32[884736]{0:T(1024)S(1)} %copy-done.1, f32[884736]{0:T(1024)} %param.15, f32[884736]{0:T(1024)} %param.16, bf16[7040,128]{1,0:T(8,128)(2,1)} %copy-done.2), kind=kLoop, calls=%fused_computation.2 | loop fusion | flops 14155776 | bytes 26542080 | tf_op jit(solution)/shard_map/sub | solution.py:99
  (262 shorter events, 33.0 us)
Async XLA Ops:
  7.2 113.4 %reduce-scatter.2.cloned.1.call-start = ((), (), s32[]{:S(2)}) async-start(), calls=%async_computation.1 | async-start | bytes 983040 | tf_op jit(solution)/shard_map/reduce_scatter | solution.py:679
  44.6 16.4 %copy-start.17 = (f32[128,576]{0,1:T(8,128)}, f32[128,576]{0,1:T(8,128)S(1)}, u32[]{:S(2)}) copy-start(f32[128,576]{0,1:T(8,128)S(1)} %copy.112) | copy-start | bytes 884740
  45.2 15.8 %copy-start.19 = (bf16[576,576]{1,0:T(8,128)(2,1)}, bf16[576,576]{1,0:T(8,128)(2,1)S(1)}, u32[]{:S(2)}) copy-start(bf16[576,576]{1,0:T(8,128)(2,1)S(1)} %reshape.496) | copy-start | bytes 1990660
  45.8 11.2 %copy-start.23 = (bf16[2,64,576]{2,1,0:T(8,128)(2,1)}, bf16[2,64,576]{2,1,0:T(8,128)(2,1)S(1)}, u32[]{:S(2)}) copy-start(bf16[2,64,576]{2,1,0:T(8,128)(2,1)S(1)} %multiply_convert_fusion.3) | copy-start | bytes 442372
  46.6 9.0 %copy-start.27 = (bf16[576,192]{1,0:T(8,128)(2,1)}, bf16[576,192]{1,0:T(8,128)(2,1)S(1)}, u32[]{:S(2)}) copy-start(bf16[576,192]{1,0:T(8,128)(2,1)S(1)} %reshape.489) | copy-start | bytes 663556
  47.8 9.6 %copy-start.55 = (f32[128,32]{0,1:T(8,128)}, f32[128,32]{0,1:T(8,128)S(1)}, u32[]{:S(2)}) copy-start(f32[128,32]{0,1:T(8,128)S(1)} %get-tuple-element.83) | copy-start | bytes 49156
  47.8 9.6 %copy-start.57 = (f32[128,32]{0,1:T(8,128)}, f32[128,32]{0,1:T(8,128)S(1)}, u32[]{:S(2)}) copy-start(f32[128,32]{0,1:T(8,128)S(1)} %get-tuple-element.84) | copy-start | bytes 49156
  55.9 4.4 %copy-start.45 = (bf16[256,192]{0,1:T(8,128)(2,1)}, bf16[256,192]{0,1:T(8,128)(2,1)S(1)}, u32[]{:S(2)}) copy-start(bf16[256,192]{0,1:T(8,128)(2,1)S(1)} %copy.109) | copy-start | bytes 294916
  58.8 3.5 %copy-start.47 = (bf16[256,192]{0,1:T(8,128)(2,1)}, bf16[256,192]{0,1:T(8,128)(2,1)S(1)}, u32[]{:S(2)}) copy-start(bf16[256,192]{0,1:T(8,128)(2,1)S(1)} %copy.103) | copy-start | bytes 294916
  58.9 3.4 %copy-start.51 = (bf16[256,192]{0,1:T(8,128)(2,1)}, bf16[256,192]{0,1:T(8,128)(2,1)S(1)}, u32[]{:S(2)}) copy-start(bf16[256,192]{0,1:T(8,128)(2,1)S(1)} %copy.104) | copy-start | bytes 294916
  59.3 3.0 %copy-start.12 = (f32[3,3,64,256]{3,2,1,0:T(8,128)}, f32[3,3,64,256]{3,2,1,0:T(8,128)S(1)}, u32[]{:S(2)}) copy-start(f32[3,3,64,256]{3,2,1,0:T(8,128)S(1)} %get-tuple-element.88) | copy-start | bytes 1769476
  89.8 4.4 %copy-start.14 = (bf16[1536,576]{1,0:T(8,128)(2,1)S(1)}, bf16[1536,576]{1,0:T(8,128)(2,1)}, u32[]{:S(2)}) copy-start(bf16[1536,576]{1,0:T(8,128)(2,1)} %reshape.499) | copy-start | bytes 5308420
  89.8 4.4 %copy-start.16 = (f32[128,576]{0,1:T(8,128)S(1)}, f32[128,576]{0,1:T(8,128)}, u32[]{:S(2)}) copy-start(f32[128,576]{0,1:T(8,128)} %get-tuple-element.90) | copy-start | bytes 884740
  94.2 4.0 %copy-start.56 = (f32[128,32]{0,1:T(8,128)S(1)}, f32[128,32]{0,1:T(8,128)}, u32[]{:S(2)}) copy-start(f32[128,32]{0,1:T(8,128)} %copy-done.55) | copy-start | bytes 49156
  94.2 4.0 %copy-start.58 = (f32[128,32]{0,1:T(8,128)S(1)}, f32[128,32]{0,1:T(8,128)}, u32[]{:S(2)}) copy-start(f32[128,32]{0,1:T(8,128)} %copy-done.57) | copy-start | bytes 49156
  94.2 4.7 %copy-start.24 = (bf16[2,64,576]{2,1,0:T(8,128)(2,1)S(1)}, bf16[2,64,576]{2,1,0:T(8,128)(2,1)}, u32[]{:S(2)}) copy-start(bf16[2,64,576]{2,1,0:T(8,128)(2,1)} %copy-done.23) | copy-start | bytes 442372
  99.3 3.7 %copy-start.26 = (bf16[128,576]{0,1:T(8,128)(2,1)S(1)}, bf16[128,576]{0,1:T(8,128)(2,1)}, u32[]{:S(2)}) copy-start(bf16[128,576]{0,1:T(8,128)(2,1)} %copy-done.25) | copy-start | bytes 442372
  104.5 3.3 %copy-start.36 = (bf16[128,1536]{1,0:T(8,128)(2,1)S(1)}, bf16[128,1536]{1,0:T(8,128)(2,1)}, u32[]{:S(2)}) copy-start(bf16[128,1536]{1,0:T(8,128)(2,1)} %copy-done.35) | copy-start | bytes 1179652
  108.4 3.0 %copy-start.38 = (bf16[128,1536]{1,0:T(8,128)(2,1)S(1)}, bf16[128,1536]{1,0:T(8,128)(2,1)}, u32[]{:S(2)}) copy-start(bf16[128,1536]{1,0:T(8,128)(2,1)} %get-tuple-element.60) | copy-start | bytes 1179652
  108.4 3.0 %copy-start.53 = (bf16[2,64,576]{2,1,0:T(8,128)(2,1)S(1)}, bf16[2,64,576]{2,1,0:T(8,128)(2,1)}, u32[]{:S(2)}) copy-start(bf16[2,64,576]{2,1,0:T(8,128)(2,1)} %param.12) | copy-start | bytes 442372
  116.1 3.1 %copy-start.62 = (bf16[576]{0:T(1024)(128)(2,1)S(1)}, bf16[576]{0:T(1024)(128)(2,1)}, u32[]{:S(2)}) copy-start(bf16[576]{0:T(1024)(128)(2,1)} %get-tuple-element.38) | copy-start | bytes 3460
  116.1 3.2 %copy-start.22 = (bf16[576,576]{1,0:T(8,128)(2,1)S(1)}, bf16[576,576]{1,0:T(8,128)(2,1)}, u32[]{:S(2)}) copy-start(bf16[576,576]{1,0:T(8,128)(2,1)} %copy-done.21) | copy-start | bytes 1990660
  116.1 4.5 %copy-start.30 = (bf16[576,192]{1,0:T(8,128)(2,1)S(1)}, bf16[576,192]{1,0:T(8,128)(2,1)}, u32[]{:S(2)}) copy-start(bf16[576,192]{1,0:T(8,128)(2,1)} %copy-done.29) | copy-start | bytes 663556
  119.1 4.1 %copy-start.18 = (f32[128,576]{0,1:T(8,128)S(1)}, f32[128,576]{0,1:T(8,128)}, u32[]{:S(2)}) copy-start(f32[128,576]{0,1:T(8,128)} %copy-done.17) | copy-start | bytes 884740
  119.1 4.1 %copy-start.60 = (f32[576]{0:T(1024)S(1)}, f32[576]{0:T(1024)}, u32[]{:S(2)}) copy-start(f32[576]{0:T(1024)} %copy-done.59) | copy-start | bytes 6916
  119.1 4.1 %copy-start.65 = (f32[128]{0:T(128)S(1)}, f32[128]{0:T(128)}, u32[]{:S(2)}) copy-start(f32[128]{0:T(128)} %rsqrt.22) | copy-start | bytes 1540
  119.1 4.5 %copy-start.28 = (bf16[576,192]{1,0:T(8,128)(2,1)S(1)}, bf16[576,192]{1,0:T(8,128)(2,1)}, u32[]{:S(2)}) copy-start(bf16[576,192]{1,0:T(8,128)(2,1)} %copy-done.27) | copy-start | bytes 663556
  136.2 79.3 %copy-start.1 = (f32[884736]{0:T(1024)S(1)}, f32[884736]{0:T(1024)}, u32[]{:S(2)}) copy-start(f32[884736]{0:T(1024)} %param.14) | copy-start | bytes 10616836
  215.5 8.4 %copy-start.64 = (f32[2,144]{1,0:T(2,128)}, f32[2,144]{1,0:T(2,128)S(1)}, u32[]{:S(2)}) copy-start(f32[2,144]{1,0:T(2,128)S(1)} %reshape.524) | copy-start | bytes 3460
  215.5 8.4 %copy-start.63 = (f32[2,144]{1,0:T(2,128)S(1)}, f32[2,144]{1,0:T(2,128)}, u32[]{:S(2)}) copy-start(f32[2,144]{1,0:T(2,128)} %param.17) | copy-start | bytes 3460
  215.5 8.4 %copy-start.69 = (f32[2,144]{1,0:T(2,128)S(1)}, f32[2,144]{1,0:T(2,128)}, u32[]{:S(2)}) copy-start(f32[2,144]{1,0:T(2,128)} %param.18) | copy-start | bytes 3460
  215.5 8.4 %copy-start.70 = (f32[2,144]{1,0:T(2,128)S(1)}, f32[2,144]{1,0:T(2,128)}, u32[]{:S(2)}) copy-start(f32[2,144]{1,0:T(2,128)} %param.19) | copy-start | bytes 3460
  (41 other events, 64.9 us)
Sparse Core Ops, SparseCore 0:
  90.9 23.6 reduce-scatter.1

commit v3 on v2

--- a/solution.py
+++ b/solution.py
@@ -30,7 +30,7 @@
 TILE = 16
 
 
-def split_weights(flat_vector):
+def split_weights(flat_vector, w_gate, w_up):
     q_width = HEADS * HEAD_DIM
     kv_width = KV_HEADS * HEAD_DIM
     layout = [(D, q_width), (D, kv_width), (D, kv_width), (q_width, D), (D, FF), (D, FF), (FF, D)]
@@ -41,8 +41,10 @@
         piece = lax.slice_in_dim(
             flat_vector, offset // LANES, (offset + amount) // LANES, axis=0
         )
-        pieces.append(lax.optimization_barrier(piece).reshape(rows_cols))
+        piece = lax.optimization_barrier(piece)
+        pieces.append(piece.reshape(rows_cols))
         offset = offset + amount
+    pieces[4], pieces[5] = w_gate, w_up
     return pieces
 
 
@@ -155,12 +157,6 @@
         [grad_key.reshape(key_rows, -1), grad_value.reshape(key_rows, -1)], axis=-1
     )
     return (grad_query, stacked)
-
-
-def cut_evenly(total_units, most):
-    count = max(1, min(most, total_units))
-    base, extra = divmod(total_units, count)
-    return [base + (1 if i < extra else 0) for i in range(count)]
 
 
 def block_of(rows):
@@ -225,7 +221,10 @@
     pl.semaphore_wait(barrier, len(targets))
 
 
-def gather_kernel(n_group, n_dp, cuts, w_ref, g_ref, out_ref, gout_ref, send_sem, recv_sem):
+def gather_kernel(
+    n_group, n_dp, cuts, w_ref, g_ref, out_ref, gout_ref, gate_ref, up_ref,
+    send_sem, recv_sem, local_sem,
+):
     me, dp = lax.axis_index("group"), lax.axis_index("dp")
     core, chip, chips = me % 2, me // 2, n_group // 2
     sib = me + 1 - 2 * core
@@ -246,7 +245,27 @@
     base_gain = base_own + n_cut + 1
     gout_ref[pl.ds(me, 1)] = g_ref[...][None]
 
+    blocks = FF // LANES
+    kind = me // (n_group // 4)
+    by_column = jnp.logical_or(kind == 1, kind == 2)
+
     def cast(start, rows):
+        @pl.when(by_column)
+        def _():
+            column = start // rows
+
+            def step(i, block):
+                out_ref[me, rows_at(start + i, block), :] = w_ref[
+                    pl.ds(i * blocks + column, block, stride=blocks), :
+                ].astype(jnp.bfloat16)
+
+            over_rows(rows, step)
+
+        @pl.when(jnp.logical_not(by_column))
+        def _():
+            cast_rows(start, rows)
+
+    def cast_rows(start, rows):
         def step(i, block):
             out_ref[me, rows_at(start + i, block), :] = w_ref[
                 rows_at(start + i, block), :
@@ -271,7 +290,8 @@
     for j in range(1, n_group):
         line = gout_ref.at[me]
         copies.start(line, line, base_gain + j - 1, at((me + j) % n_group, dp))
-    cast(theirs, half_rows)
+    for c in range(n_cut):
+        cast(theirs + starts[c], cuts[c])
     rest = out_ref.at[me, rows_at(theirs, half_rows), :]
     copies.start(rest, rest, base_own + n_cut, at(sib, dp))
     for c in range(n_cut + 1):
@@ -304,12 +324,29 @@
     for j in range(1, n_group):
         source = (me + n_group - j) % n_group
         copies.arrived(gout_ref.at[source], base_gain + j - 1, at(source, dp))
+    parts = n_group // 4
+    depth = w_ref.shape[0] // blocks
+    local = []
+    for number, matrix in enumerate((gate_ref, up_ref)):
+        for part in range(parts):
+            for column in range(blocks):
+                local.append(
+                    pltpu.make_async_copy(
+                        out_ref.at[(number + 1) * parts + part, pl.ds(column * depth, depth), :],
+                        matrix.at[pl.ds(part * depth, depth), pl.ds(column * LANES, LANES)],
+                        local_sem.at[len(local)],
+                    )
+                )
+    for copy in local:
+        copy.start()
+    for copy in local:
+        copy.wait()
     copies.finish()
 
 
 def gather_weights(weights, gains, n_group, n_dp):
     rows = weights.shape[0] // LANES
-    cuts = [units * TILE for units in cut_evenly(rows // 2 // TILE, 4)]
+    cuts = [rows * LANES // FF] * (FF // LANES // 2)
     gain_size = gains.shape[0] * gains.shape[1]
     gain_tile = (
         jnp.zeros((TILE * LANES,), jnp.bfloat16)
@@ -320,27 +357,34 @@
     far = n_group // 2 - 1
     slots = 4 * far * len(cuts) + len(cuts) + 1 + n_group - 1
     vmem = pl.BlockSpec(memory_space=pltpu.VMEM)
-    full, full_gains = pl.pallas_call(
+    full, full_gains, w_gate, w_up = pl.pallas_call(
         functools.partial(gather_kernel, n_group, n_dp, cuts),
         out_shape=(
             jax.ShapeDtypeStruct((n_group, rows, LANES), jnp.bfloat16),
             jax.ShapeDtypeStruct((n_group, TILE, LANES), jnp.bfloat16),
+            jax.ShapeDtypeStruct((D, FF), jnp.bfloat16),
+            jax.ShapeDtypeStruct((D, FF), jnp.bfloat16),
         ),
         in_specs=[vmem, vmem],
-        out_specs=(vmem, vmem),
-        scratch_shapes=[pltpu.SemaphoreType.DMA((slots,)), pltpu.SemaphoreType.DMA((slots,))],
+        out_specs=(vmem, vmem, vmem, vmem),
+        scratch_shapes=[
+            pltpu.SemaphoreType.DMA((slots,)),
+            pltpu.SemaphoreType.DMA((slots,)),
+            pltpu.SemaphoreType.DMA((2 * (n_group // 4) * FF // LANES,)),
+        ],
         compiler_params=pltpu.CompilerParams(
             collective_id=0, has_side_effects=True, vmem_limit_bytes=16 * 1024 * 1024
         ),
     )(weights.reshape(rows, LANES), gain_tile)
     full_gains = full_gains.reshape(n_group, -1)[:, :gain_size]
     full_gains = full_gains.reshape(n_group, gains.shape[0], gains.shape[1])
-    return full.reshape(-1, LANES), full_gains.transpose(1, 0, 2).reshape(gains.shape[0], -1)
+    full_gains = full_gains.transpose(1, 0, 2).reshape(gains.shape[0], -1)
+    return full.reshape(-1, LANES), full_gains, w_gate, w_up
 
 
 def reduce_kernel(n_group, n_dp, cuts, moves, *refs):
     pieces = refs[: 1 + max(move[0] for move in moves)]
-    (gain_ref, out_ref, src, buf1, buf2, sum2, buf3, sum3, buf4, send_sem, recv_sem, local_sem) = refs[
+    (gain_ref, result_ref, src, out_ref, buf1, buf2, sum2, buf3, sum3, buf4, send_sem, recv_sem, local_sem) = refs[
         len(pieces) :
     ]
     me, dp = lax.axis_index("group"), lax.axis_index("dp")
@@ -353,10 +397,10 @@
     far_to = [((chip + j) % chips) * 2 + core for j in range(1, chips)]
     line_to = [((place + j) % places) * 2 + half for j in range(1, places)]
     local = []
-    for number, (piece, first, rank, row, rows) in enumerate(moves):
+    for number, (piece, first, column, rank, row, rows) in enumerate(moves):
         local.append(
             pltpu.make_async_copy(
-                pieces[piece].at[pl.ds(first, rows), :],
+                pieces[piece].at[pl.ds(first, rows), pl.ds(column, LANES)],
                 src.at[rank // 2, rank % 2, pl.ds(row, rows), :],
                 local_sem.at[number],
             )
@@ -502,6 +546,34 @@
         for stage, lag in zip(stages, lags):
             if 0 <= t - lag < n_cut:
                 stage(t - lag)
+    blocks = FF // LANES
+    kind = me // (n_group // 4)
+    by_column = jnp.logical_or(kind == 1, kind == 2)
+    shard_rows = src.shape[2] - gain_rows
+    depth = shard_rows // blocks
+
+    @pl.when(by_column)
+    def _():
+        for column in range(blocks):
+
+            def step(i, block):
+                result_ref[pl.ds(i * blocks + column, block, stride=blocks), :] = out_ref[
+                    rows_at(column * depth + i, block), :
+                ].astype(f32)
+
+            over_rows(depth, step)
+
+    @pl.when(jnp.logical_not(by_column))
+    def _():
+        def step(i, block):
+            here = rows_at(i, block)
+            result_ref[here, :] = out_ref[here, :].astype(f32)
+
+        over_rows(shard_rows, step)
+
+    result_ref[pl.ds(shard_rows, gain_rows), :] = out_ref[
+        pl.ds(shard_rows, gain_rows), :
+    ].astype(f32)
     copies.finish()
 
 
@@ -516,8 +588,9 @@
 
 
 def reduce_grads(weight_parts, gain_grad, n_group, n_dp):
-    pieces = [part.astype(jnp.bfloat16).reshape(-1, LANES) for part in weight_parts]
-    shard_rows = sum(piece.shape[0] for piece in pieces) // n_group
+    pieces = [part.astype(jnp.bfloat16) for part in weight_parts]
+    pieces = [part if part.shape == (D, FF) else part.reshape(-1, LANES) for part in pieces]
+    shard_rows = sum(piece.size for piece in pieces) // n_group // LANES
     unit = TILE * n_dp
     main_units = shard_rows // unit
     main_rows = main_units * unit
@@ -538,24 +611,41 @@
     moves = []
     begin = 0
     for number, piece in enumerate(pieces):
-        first, end = begin, begin + piece.shape[0]
+        first, end = begin, begin + piece.size // LANES
+        while first < end and piece.shape == (D, FF):
+            depth = shard_rows * LANES // FF
+            for column in range(FF // LANES):
+                moves.append(
+                    (
+                        number,
+                        (first - begin) * LANES // FF,
+                        column * LANES,
+                        first // shard_rows,
+                        column * depth,
+                        depth,
+                    )
+                )
+            first += shard_rows
         while first < end:
             rank = first // shard_rows
             stop = min(end, (rank + 1) * shard_rows)
-            moves.append((number, first - begin, rank, first - rank * shard_rows, stop - first))
+            moves.append(
+                (number, first - begin, 0, rank, first - rank * shard_rows, stop - first)
+            )
             first = stop
         begin = end
     slots = len(cuts) * (3 + (chips - 1) + 2 * (places - 1))
     vmem = pl.BlockSpec(memory_space=pltpu.VMEM)
-    anywhere = pl.BlockSpec(memory_space=pl.ANY)
+    anywhere = pl.BlockSpec(memory_space=pltpu.HBM)
     bf16 = jnp.bfloat16
     out = pl.pallas_call(
         functools.partial(reduce_kernel, n_group, n_dp, cuts, moves),
-        out_shape=jax.ShapeDtypeStruct((total_rows, LANES), bf16),
+        out_shape=jax.ShapeDtypeStruct((total_rows, LANES), jnp.float32),
         in_specs=[anywhere] * (len(pieces) + 1),
         out_specs=vmem,
         scratch_shapes=[
             pltpu.VMEM((chips, 2, total_rows, LANES), bf16),
+            pltpu.VMEM((total_rows, LANES), bf16),
             pltpu.VMEM((chips, total_rows, LANES), bf16),
             pltpu.VMEM((chips - 1, total_rows, LANES), bf16),
             pltpu.VMEM((total_rows, LANES), bf16),
@@ -567,12 +657,12 @@
             pltpu.SemaphoreType.DMA((len(moves) + 1,)),
         ],
         compiler_params=pltpu.CompilerParams(
-            collective_id=1, has_side_effects=True, vmem_limit_bytes=22 * 1024 * 1024
+            collective_id=1, has_side_effects=True, vmem_limit_bytes=26 * 1024 * 1024
         ),
     )(*pieces, gain_flat.reshape(chips, 2, tail_rows - spare, LANES))
-    grad_shard = out[:shard_rows].reshape(-1).astype(jnp.float32)
+    grad_shard = out[:shard_rows].reshape(-1)
     gain_shard = out[shard_rows : shard_rows + gain_rows].reshape(-1)[:gain_size]
-    return grad_shard, gain_shard.reshape(-1, gain_cols).astype(jnp.float32)
+    return grad_shard, gain_shard.reshape(-1, gain_cols)
 
 
 def body(
@@ -595,8 +685,8 @@
     q_width = HEADS * HEAD_DIM
     kv_width = KV_HEADS * HEAD_DIM
     group_size = HEADS // KV_HEADS
-    full_flat, full_gains = gather_weights(weights, gains, n_group, n_dp)
-    w_query, w_key, w_value, w_out, w_gate, w_up, w_down = split_weights(full_flat)
+    full_flat, full_gains, gathered_gate, gathered_up = gather_weights(weights, gains, n_group, n_dp)
+    w_query, w_key, w_value, w_out, w_gate, w_up, w_down = split_weights(full_flat, gathered_gate, gathered_up)
     gain_attn = full_gains[0].astype(jnp.float32)
     gain_ffn = full_gains[1].astype(jnp.float32)
     offsets = jnp.arange(SPAN, dtype=jnp.int32)

time: 232 us -> 286 us (1.23)
  local copies, waits for them, and re-layouts: 56.9 us -> 84.1 us
  other arithmetic: 16 us -> 30.5 us
  matrix products: 26.8 us -> 38.1 us
    reshape x14 -> x11, local copies, waits for them, and re-layouts: 27.6 us -> 21.2 us  [the longest x5 12.8 us: split_weights(): pieces.append(piece.reshape(rows_cols))]
    slice x4, local copies, waits for them, and re-layouts: 0.41 us -> 5.81 us  [split_pair(): key_blk = kv_seq[:, :kv_width].reshape(-1, KV_HEADS, HEAD_DIM)]
    le x3, local copies, waits for them, and re-layouts: 0.16 us -> 3.92 us  [masked_scores(): allowed = key_pos[None, :] <= query_pos[:, None]]
    dot_general x7, matrix products: 5.43 us -> 8.82 us  [outer_sum(): lax.dot_general(left_rows, right_rows, (((0,), (0,)), ((), ())), preferre...]
    slice x2, local copies, waits for them, and re-layouts: 0.2 us -> 3.3 us  [split_pair(): value_blk = kv_seq[:, kv_width:].reshape(-1, KV_HEADS, HEAD_DIM)]
    concatenate x2, local copies, waits for them, and re-layouts: 0.28 us -> 3.34 us  [body(): jnp.concatenate([key_b, value_b], axis=-1)]
    unnamed x147 -> x129, local copies, waits for them, and re-layouts: 13.7 us -> 16.1 us
  transfers between devices with their start and end apart: 1 -> 1, of which waited for: 0 -> 0; matrix products, arithmetic and copies ran while one was open for 13% -> 9% of each run, Pallas kernels for 0% -> 0%
where the time goes in v3:
time: 286 us; the launch traced here: 284 us
  Pallas kernels  109 us (38%)
  local copies, waits for them, and re-layouts  84.1 us (29%)
  matrix products  38.1 us (13%)
  other arithmetic  30.5 us (11%)
  between operations  14.9 us (5%)
  blocking collectives  7.51 us (3%)
    pallas_call x1, Pallas kernels, reduce_grads(): pl.pallas_call(functools.partial(reduce_kernel, n_group, n_dp, cuts, move...  78.6 us
    pallas_call x1, Pallas kernels, gather_weights(): pl.pallas_call(functools.partial(gather_kernel, n_group, n_dp, cuts), out...  30.4 us
    unnamed x129, local copies, waits for them, and re-layouts  16.1 us
    reshape x5, local copies, waits for them, and re-layouts, split_weights(): pieces.append(piece.reshape(rows_cols))  12.8 us
    dot_general x7, matrix products, outer_sum(): lax.dot_general(left_rows, right_rows, (((0,), (0,)), ((), ())), preferre...  8.82 us
    sub x2, other arithmetic, adamw_step(): param_now - step_rate * (update + decay_weight * param_now)  8.7 us
    reshape x5, local copies, waits for them, and re-layouts, reduce_grads(): part.reshape(-1, LANES)  8.37 us
    all_gather x1, blocking collectives, body(): kv_all = lax.all_gather(kv_local, 'group', axis=1, tiled=True)  7.51 us
  transfers between devices with their start and end apart: 1, of which 0 were waited for; matrix products, arithmetic and copies ran while one was open for 9% of the time, Pallas kernels for 0%

profile of v3, /device:TPU:0, one launch (start us, length us, event | category | flops | bytes accessed | tf_op | source)
XLA Modules:
  0.0 284.2 jit_solution(17130157711083619171)
XLA Ops:
  8.0 2.0 copy-done.1
  10.0 30.4 %shard_map.168 = (bf16[4,6912,128]{2,1,0:T(8,128)(2,1)S(1)}, bf16[4,16,128]{2,1,0:T(8,128)(2,1)S(1)}, bf16[576,1536]{1,0:T(8,128)(2,1)S(1)}, bf16[576,1536]{1,0:T(8,128)(2,1)S(1)}) custom-call(f32[6912,128]{1,0:T(8,128)S(1)} %bitcast.209, bf16[16,128]{1,0:T(8,128)(2,1)S(1)} %pad_bitcast_fusion.1.g_ref), custom_call_target="tpu_custom_call" | custom-call | tf_op jit(solution)/shard_map/pallas_call | solution.py:360
  44.9 1.7 copy.112
  46.7 2.4 reshape.482
  50.6 1.9 reshape.476
  54.1 1.9 convolution_convert_fusion.10
  59.2 1.9 reshape.475
  61.0 1.8 copy.97
  71.8 1.9 pad_maximum_fusion.2
  73.8 1.7 copy.101
  75.5 7.5 %all_gather.4 = bf16[2,256,384]{2,0,1:T(2,128)(2,1)S(1)} all-gather(bf16[2,64,384]{2,0,1:T(2,128)(2,1)} %copy.101), channel_id=1, replica_groups=mesh['dp'=8,'group'=4] {'group'}, dimensions={1}, use_global_device_ids=true | all-gather | bytes 491520 | tf_op jit(solution)/shard_map/all_gather | solution.py:710
  85.1 1.7 copy.109
  86.7 1.7 copy.110
  88.4 2.4 reshape.479
  90.7 2.3 copy.105
  101.2 1.7 slice_maximum_fusion
  107.3 1.7 fusion.40
  110.7 1.7 copy.104
  119.6 1.8 multiply_reduce_fusion.5
  125.8 4.3 %reshape.483 = bf16[1536,576]{1,0:T(8,128)(2,1)} reshape(bf16[6912,128]{1,0:T(8,128)(2,1)} %slice_bitcast_fusion.1) | data formatting | bytes 3538944 | tf_op jit(solution)/shard_map/reshape | solution.py:45
  130.0 1.7 copy.114
  131.7 3.7 %multiply_convert_fusion = (bf16[128,1536]{1,0:T(8,128)(2,1)S(1)}, bf16[128,1536]{1,0:T(8,128)(2,1)S(1)}, bf16[128,1536]{1,0:T(8,128)(2,1)}) fusion(f32[128,1536]{1,0:T(8,128)} %fusion.48, f32[128,1536]{1,0:T(8,128)} %fusion.49, bf16[1536,576]{1,0:T(8,128)(2,1)} %reshape.483, bf16[128,576]{1,0:T(8,128)(2,1)} %bitcast.257), kind=kOutput, calls=%fused_computation.42 | convolution fusion | flops 229638144 | bytes 4669440 | tf_op jit(solution)/shard_map/dot_general | solution.py:731
  148.7 1.8 convolution_bitcast_fusion.4
  150.6 1.8 convolution_add_fusion.2
  158.8 1.9 convolution_convert_fusion
  160.6 2.8 copy.127
  163.5 3.0 %reshape.498.refs_6_ = bf16[6912,128]{1,0:T(8,128)(2,1)} reshape(bf16[1536,576]{1,0:T(8,128)(2,1)S(1)} %copy.127) | data formatting | bytes 3538944 | tf_op jit(solution)/shard_map/reshape | solution.py:592
  167.0 2.9 %convolution_convert_fusion.2.refs_4_ = bf16[576,1536]{1,0:T(8,128)(2,1)} fusion(bf16[128,576]{0,1:T(8,128)(2,1)S(1)} %copy-done.24, bf16[128,1536]{1,0:T(8,128)(2,1)} %copy-done.35), kind=kOutput, calls=%fused_computation.7 | convolution fusion | flops 227377152 | bytes 2310144 | tf_op jit(solution)/shard_map/dot_general | solution.py:92
  169.9 1.8 convolution_convert_fusion.1.refs_5_
  188.1 78.6 %shard_map.169 = f32[7040,128]{1,0:T(8,128)S(1)} custom-call(bf16[2592,128]{1,0:T(8,128)(2,1)S(1)} %copy-done.6, bf16[864,128]{1,0:T(8,128)(2,1)S(1)} %copy-done.8, bf16[864,128]{1,0:T(8,128)(2,1)S(1)} %copy-done.9, bf16[2592,128]{1,0:T(8,128)(2,1)S(1)} %copy-done.7, bf16[576,1536]{1,0:T(8,128)(2,1)S(1)} %copy-done.4, bf16[576,1536]{1,0:T(8,128)(2,1)S(1)} %copy-done.5, ...), custom_call_target="tpu_custom_call" | custom-call | tf_op jit(solution)/shard_map/pallas_call | solution.py:641
  266.8 1.8 copy-done
  268.7 8.1 %multiply_subtract_fusion = (f32[884736]{0:T(1024)}, f32[884736]{0:T(1024)}, f32[884736]{0:T(1024)}, f32[884736]{0:T(1024)}) fusion(f32[884736]{0:T(1024)S(1)} %copy-done.2, f32[884736]{0:T(1024)} %param.15, f32[884736]{0:T(1024)} %param.16, f32[7040,128]{1,0:T(8,128)} %copy-done), kind=kLoop, calls=%fused_computation.2 | loop fusion | flops 13271040 | bytes 28311552 | tf_op jit(solution)/shard_map/sub | solution.py:101
  (239 shorter events, 85.1 us)
Async XLA Ops:
  7.2 164.5 %reduce-scatter.2.cloned.1.call-start = ((), (), s32[]{:S(2)}) async-start(), calls=%async_computation.1 | async-start | bytes 983040 | tf_op jit(solution)/shard_map/reduce_scatter | solution.py:769
  49.9 17.1 %copy-start.49 = (f32[576]{0:T(1024)}, f32[576]{0:T(1024)S(1)}, u32[]{:S(2)}) copy-start(f32[576]{0:T(1024)S(1)} %reshape.505) | copy-start | bytes 6916
  50.6 10.5 %copy-start.59 = (f32[2,64]{1,0:T(2,128)}, f32[2,64]{1,0:T(2,128)S(1)}, u32[]{:S(2)}) copy-start(f32[2,64]{1,0:T(2,128)S(1)} %add_rsqrt_fusion) | copy-start | bytes 1540
  131.7 4.3 %copy-start.16 = (f32[128,576]{0,1:T(8,128)S(1)}, f32[128,576]{0,1:T(8,128)}, u32[]{:S(2)}) copy-start(f32[128,576]{0,1:T(8,128)} %copy-done.15) | copy-start | bytes 884740
  131.7 4.3 %copy-start.53 = (f32[576]{0:T(1024)S(1)}, f32[576]{0:T(1024)}, u32[]{:S(2)}) copy-start(f32[576]{0:T(1024)} %reshape.506) | copy-start | bytes 6916
  131.7 4.4 %copy-start.58 = (f32[128]{0:T(128)S(1)}, f32[128]{0:T(128)}, u32[]{:S(2)}) copy-start(f32[128]{0:T(128)} %copy-done.57) | copy-start | bytes 1540
  137.0 4.3 %copy-start.31 = (bf16[3,64,3,64]{3,1,2,0:T(8,128)(2,1)S(1)}, bf16[3,64,3,64]{3,1,2,0:T(8,128)(2,1)}, u32[]{:S(2)}) copy-start(bf16[3,64,3,64]{3,1,2,0:T(8,128)(2,1)} %copy-done.30) | copy-start | bytes 221188
  137.1 4.4 %copy-start.43 = (bf16[256,192]{0,1:T(8,128)(2,1)S(1)}, bf16[256,192]{0,1:T(8,128)(2,1)}, u32[]{:S(2)}) copy-start(bf16[256,192]{0,1:T(8,128)(2,1)} %copy.103) | copy-start | bytes 294916
  140.5 6.7 %copy-start.60 = (f32[2,64]{1,0:T(2,128)S(1)}, f32[2,64]{1,0:T(2,128)}, u32[]{:S(2)}) copy-start(f32[2,64]{1,0:T(2,128)} %copy-done.59) | copy-start | bytes 1540
  140.5 7.3 %copy-start.44 = (bf16[256,192]{0,1:T(8,128)(2,1)S(1)}, bf16[256,192]{0,1:T(8,128)(2,1)}, u32[]{:S(2)}) copy-start(bf16[256,192]{0,1:T(8,128)(2,1)} %copy.110) | copy-start | bytes 294916
  141.7 8.8 %copy-start.14 = (bf16[1536,576]{1,0:T(8,128)(2,1)S(1)}, bf16[1536,576]{1,0:T(8,128)(2,1)}, u32[]{:S(2)}) copy-start(bf16[1536,576]{1,0:T(8,128)(2,1)} %reshape.483) | copy-start | bytes 5308420
  141.8 8.8 %copy-start.17 = (f32[128,576]{0,1:T(8,128)S(1)}, f32[128,576]{0,1:T(8,128)}, u32[]{:S(2)}) copy-start(f32[128,576]{0,1:T(8,128)} %copy-done.15) | copy-start | bytes 884740
  147.2 7.4 %copy-start.48 = (f32[128,32]{0,1:T(8,128)S(1)}, f32[128,32]{0,1:T(8,128)}, u32[]{:S(2)}) copy-start(f32[128,32]{0,1:T(8,128)} %copy-done.47) | copy-start | bytes 49156
  147.2 7.5 %copy-start.22 = (bf16[2,64,576]{2,1,0:T(8,128)(2,1)S(1)}, bf16[2,64,576]{2,1,0:T(8,128)(2,1)}, u32[]{:S(2)}) copy-start(bf16[2,64,576]{2,1,0:T(8,128)(2,1)} %copy-done.21) | copy-start | bytes 442372
  150.6 6.1 %copy-start.29 = (bf16[3,64,3,64]{3,1,2,0:T(8,128)(2,1)S(1)}, bf16[3,64,3,64]{3,1,2,0:T(8,128)(2,1)}, u32[]{:S(2)}) copy-start(bf16[3,64,3,64]{3,1,2,0:T(8,128)(2,1)} %copy-done.27) | copy-start | bytes 221188
  150.6 6.1 %copy-start.32 = (bf16[3,64,3,64]{3,1,2,0:T(8,128)(2,1)S(1)}, bf16[3,64,3,64]{3,1,2,0:T(8,128)(2,1)}, u32[]{:S(2)}) copy-start(bf16[3,64,3,64]{3,1,2,0:T(8,128)(2,1)} %copy-done.30) | copy-start | bytes 221188
  153.3 5.4 %copy-start.36 = (bf16[128,1536]{1,0:T(8,128)(2,1)S(1)}, bf16[128,1536]{1,0:T(8,128)(2,1)}, u32[]{:S(2)}) copy-start(bf16[128,1536]{1,0:T(8,128)(2,1)} %get-tuple-element.61) | copy-start | bytes 1179652
  153.3 5.4 %copy-start.45 = (bf16[2,64,576]{2,1,0:T(8,128)(2,1)S(1)}, bf16[2,64,576]{2,1,0:T(8,128)(2,1)}, u32[]{:S(2)}) copy-start(bf16[2,64,576]{2,1,0:T(8,128)(2,1)} %param.12) | copy-start | bytes 442372
  154.7 4.1 %copy-start.38 = (bf16[128,9,64]{0,2,1:T(8,128)(2,1)}, bf16[128,9,64]{0,2,1:T(8,128)(2,1)S(1)}, u32[]{:S(2)}) copy-start(bf16[128,9,64]{0,2,1:T(8,128)(2,1)S(1)} %pad_maximum_fusion.5) | copy-start | bytes 442372
  160.6 5.9 %copy-start.20 = (bf16[576,576]{1,0:T(8,128)(2,1)S(1)}, bf16[576,576]{1,0:T(8,128)(2,1)}, u32[]{:S(2)}) copy-start(bf16[576,576]{1,0:T(8,128)(2,1)} %reshape.479) | copy-start | bytes 1990660
  160.6 5.9 %copy-start.39 = (bf16[128,9,64]{0,2,1:T(8,128)(2,1)S(1)}, bf16[128,9,64]{0,2,1:T(8,128)(2,1)}, u32[]{:S(2)}) copy-start(bf16[128,9,64]{0,2,1:T(8,128)(2,1)} %copy-done.38) | copy-start | bytes 442372
  160.6 6.3 %copy-start.24 = (bf16[128,576]{0,1:T(8,128)(2,1)S(1)}, bf16[128,576]{0,1:T(8,128)(2,1)}, u32[]{:S(2)}) copy-start(bf16[128,576]{0,1:T(8,128)(2,1)} %copy-done.23) | copy-start | bytes 442372
  166.5 5.2 %copy-start.26 = (bf16[576,192]{1,0:T(8,128)(2,1)S(1)}, bf16[576,192]{1,0:T(8,128)(2,1)}, u32[]{:S(2)}) copy-start(bf16[576,192]{1,0:T(8,128)(2,1)} %reshape.476) | copy-start | bytes 663556
  167.0 7.2 %copy-start.18 = (f32[128,576]{0,1:T(8,128)S(1)}, f32[128,576]{0,1:T(8,128)}, u32[]{:S(2)}) copy-start(f32[128,576]{0,1:T(8,128)} %copy.112) | copy-start | bytes 884740
  167.0 7.2 %copy-start.50 = (f32[576]{0:T(1024)S(1)}, f32[576]{0:T(1024)}, u32[]{:S(2)}) copy-start(f32[576]{0:T(1024)} %copy-done.49) | copy-start | bytes 6916
  167.0 7.2 %copy-start.56 = (f32[128]{0:T(128)S(1)}, f32[128]{0:T(128)}, u32[]{:S(2)}) copy-start(f32[128]{0:T(128)} %rsqrt.22) | copy-start | bytes 1540
  167.0 8.5 %copy-start.25 = (bf16[576,192]{1,0:T(8,128)(2,1)S(1)}, bf16[576,192]{1,0:T(8,128)(2,1)}, u32[]{:S(2)}) copy-start(bf16[576,192]{1,0:T(8,128)(2,1)} %reshape.475) | copy-start | bytes 663556
  188.1 80.5 %copy-start.2 = (f32[884736]{0:T(1024)S(1)}, f32[884736]{0:T(1024)}, u32[]{:S(2)}) copy-start(f32[884736]{0:T(1024)} %param.14) | copy-start | bytes 10616836
  268.6 8.1 %copy-start.55 = (f32[2,144]{1,0:T(2,128)}, f32[2,144]{1,0:T(2,128)S(1)}, u32[]{:S(2)}) copy-start(f32[2,144]{1,0:T(2,128)S(1)} %reshape.503) | copy-start | bytes 3460
  268.6 8.1 %copy-start.54 = (f32[2,144]{1,0:T(2,128)S(1)}, f32[2,144]{1,0:T(2,128)}, u32[]{:S(2)}) copy-start(f32[2,144]{1,0:T(2,128)} %param.17) | copy-start | bytes 3460
  268.6 8.1 %copy-start.61 = (f32[2,144]{1,0:T(2,128)S(1)}, f32[2,144]{1,0:T(2,128)}, u32[]{:S(2)}) copy-start(f32[2,144]{1,0:T(2,128)} %param.18) | copy-start | bytes 3460
  268.6 8.1 %copy-start.62 = (f32[2,144]{1,0:T(2,128)S(1)}, f32[2,144]{1,0:T(2,128)}, u32[]{:S(2)}) copy-start(f32[2,144]{1,0:T(2,128)} %param.19) | copy-start | bytes 3460
  (32 other events, 60.2 us)
Sparse Core Ops, SparseCore 0:
  147.3 23.6 reduce-scatter.1
